TPU v7x, 256 devices: a whole 4x4x8 slice. The times are simulated.
256 devices in a mesh: tile: 128 (over z, x_lo, y, core), lev: 2 (over x_hi).
Axes of the slice: x: 4 (x_hi: 2, x_lo: 2; x = x_hi * 2 + x_lo), y: 4, z: 8, core: 2. Of those that a mesh axis runs over, the one named last changes fastest.
Arguments:
- tracers: float32 [2, 2048, 64, 384], P(None, 'tile', 'lev'), may hold values from -6 to 6
- zonal_courant: float32 [2048, 64, 384], P('tile', 'lev'), may hold values from -0.9 to 0.9
- merid_courant: float32 [2048, 64, 384], P('tile', 'lev'), may hold values from -0.9 to 0.9
- vertical_courant: float32 [2048, 64, 384], P('tile', 'lev'), may hold values from -0.9 to 0.9
- diffusivity: float32 [2048, 64, 384], P('tile', 'lev'), may hold values from 0.05 to 0.5
- turbulence: float32 [2048, 64, 384], P('tile', 'lev'), may hold values from 4 to 4000000
- sea_column: int32 [2048, 384], P('tile'), may hold values 0 or 1
- bottom_level: int32 [2048, 384], P('tile'), may hold values from 0 to 63
Outputs:
- updated: float32 [2, 2048, 64, 384], P(None, 'tile', 'lev')
All inputs are finite; a program needn't handle non-finite values. No bound on the sum of `sea_column` on one device may be relied on, other than what follows from the above.
Results may differ from a plain program's by a relative error of at most 0.0003.
Values sent between devices are 32-bit elements; how exact they have to be, the bound alone decides.
No kernel may reach another device: no remote copies, remote signals or barrier semaphores. Data moves between devices by JAX's collectives and lax.ppermute only.
A program may use at most 64 MiB of HBM per device.

v0:
```python
import jax
import jax.numpy as jnp
from jax import lax
from jax.experimental import pallas as pl
from jax.experimental.pallas import tpu as pltpu
from jax.sharding import PartitionSpec as P

thermal_coef = 0.2
haline_coef = 0.8
taper_eps = 0.05

X = 16
K = 32
Y = 384
LANES = 3
FAR = 1 << 20
F32 = jnp.float32


def any_spec():
    return pl.BlockSpec(memory_space=pl.ANY)


def vmem_spec():
    return pl.BlockSpec(memory_space=pltpu.VMEM)


def run_copies(copies):
    for copy in copies:
        copy.start()
    for copy in copies:
        copy.wait()


def face_flux(courant, behind, in_front, grad, back, front):
    half = 0.5 * courant
    speed = jnp.abs(courant)
    half_speed = jnp.abs(half)
    weight = half_speed * (1.0 - speed)
    forward = courant > 0.0
    fluxes = []
    for t in range(2):
        upwind = jnp.where(forward, back[t], front[t])
        rising = grad[t] > 0.0
        size = jnp.abs(grad[t])
        along = jnp.where(rising, upwind, -upwind)
        limited = jnp.maximum(
            jnp.minimum(2.0 * jnp.minimum(size, along), jnp.maximum(size, along)), 0.0
        )
        limited = jnp.where(rising, limited, -limited)
        fluxes.append(half * (behind[t] + in_front[t]) - half_speed * grad[t] + weight * limited)
    return fluxes


def isoneutral(grad, vert, coeff):
    dens_side = haline_coef * grad[1] - thermal_coef * grad[0]
    dens_vert = haline_coef * vert[1] - thermal_coef * vert[0]
    slope = dens_side * dens_vert / (dens_vert * dens_vert + taper_eps)
    return [coeff * (grad[t] - slope * vert[t]) for t in range(2)]


def lane_roll(values, shift):
    return pltpu.roll(values, shift % Y, 1)


def row_roll(values, shift):
    return pltpu.roll(values, shift % values.shape[0], 0)


def south_depth(depth):
    lane = lax.broadcasted_iota(jnp.int32, depth.shape, 1)
    return jnp.where(lane == 0, 0, jnp.minimum(depth, lane_roll(depth, 1)))


def west_depth(depth):
    return jnp.minimum(depth, row_roll(depth, 1))


def pack_kernel(
    tracers, zonal, vertical, diffusivity, turbulence, sea, bottom,
    east_msg, west_msg, level_msg, east_corner, west_corner, depth_rows, sems
):
    slab = lax.axis_index("lev")
    edge = (K - 1) * (1 - slab)
    first = (K - 2) * (1 - slab)
    copies = []

    def add(src, dst):
        copies.append(pltpu.make_async_copy(src, dst, sems.at[len(copies)]))
        copies[-1].start()

    for t in range(2):
        for i in range(2):
            rows = pl.ds((2 * t + i) * K, K)
            add(tracers.at[t, X - 2 + i], east_msg.at[rows])
            add(tracers.at[t, i], west_msg.at[rows])
            add(tracers.at[t, :, first + i, :], level_msg.at[2 * t + i])
        add(tracers.at[t, X - 1, edge, :], east_corner.at[t])
        add(tracers.at[t, 0, edge, :], west_corner.at[t])
    add(zonal.at[0], west_msg.at[pl.ds(4 * K, K)])
    add(diffusivity.at[0], west_msg.at[pl.ds(5 * K, K)])
    fifth = len(copies)
    upper = pltpu.make_async_copy(turbulence.at[:, K - 1, :], level_msg.at[4], sems.at[fifth])
    lower = pltpu.make_async_copy(vertical.at[:, 0, :], level_msg.at[4], sems.at[fifth])

    @pl.when(slab == 0)
    def _():
        upper.start()

    @pl.when(slab == 1)
    def _():
        lower.start()

    depth_rows[...] = (sea[...] * (bottom[...] + 1)).astype(F32)
    last = [
        pltpu.make_async_copy(depth_rows.at[pl.ds(8, 8)], east_msg.at[pl.ds(4 * K, 8)], sems.at[fifth + 1]),
        pltpu.make_async_copy(depth_rows.at[pl.ds(0, 8)], west_msg.at[pl.ds(6 * K, 8)], sems.at[fifth + 2]),
    ]
    for copy in last:
        copy.start()
    upper.wait()
    for copy in copies + last:
        copy.wait()


def interior_kernel(
    tracers, zonal, merid, vertical, diffusivity, turbulence, sea, bottom,
    p_out, inverse_out, carry_out, ratio_out, tail_out,
    q, zc, mc, vc, df, tb, below_flux, rate, sems
):
    slab = lax.axis_index("lev")
    edge = (K - 1) * (1 - slab)
    base = K * slab

    def copies(k):
        pairs = [
            (tracers.at[0, :, k, :], q.at[0, k]),
            (tracers.at[1, :, k, :], q.at[1, k]),
            (zonal.at[:, k, :], zc.at[k]),
            (merid.at[:, k, :], mc.at[k]),
            (vertical.at[:, k, :], vc.at[k]),
            (diffusivity.at[:, k, :], df.at[k]),
            (turbulence.at[:, k, :], tb.at[k]),
        ]
        return [pltpu.make_async_copy(a, b, sems.at[i, k]) for i, (a, b) in enumerate(pairs)]

    @pl.loop(0, K)
    def _(k):
        for copy in copies(k):
            copy.start()

    depth = sea[...] * (bottom[...] + 1)
    depth_west = west_depth(depth)
    row = lax.broadcasted_iota(jnp.int32, (X, Y), 0)
    depth_west_inner = jnp.where((row >= 2) & (row <= X - 2), depth_west, 0)
    depth_south = south_depth(depth)
    below_flux[...] = jnp.zeros_like(below_flux)
    rate[0] = jnp.zeros((X, Y), F32)

    for k in range(2):
        for copy in copies(k):
            copy.wait()

    @pl.loop(0, K)
    def _(k):
        ahead = jnp.minimum(k + 2, K - 1)

        @pl.when(k + 2 < K)
        def _():
            for copy in copies(ahead):
                copy.wait()

        level = base + k
        up = jnp.maximum(k - 1, 0)
        down = jnp.minimum(k + 1, K - 1)
        here = [q[t, k] for t in range(2)]
        next_row = [q[t, down] for t in range(2)]
        open_up = jnp.where(k > 0, level, FAR) < depth
        open_down = jnp.where(k < K - 1, level + 1, FAR) < depth
        open_far = jnp.where(k < K - 2, level + 2, FAR) < depth
        grad_up = [jnp.where(open_up, here[t] - q[t, up], 0.0) for t in range(2)]
        grad_down = [jnp.where(open_down, next_row[t] - here[t], 0.0) for t in range(2)]
        grad_far = [jnp.where(open_far, q[t, ahead] - next_row[t], 0.0) for t in range(2)]
        centred = [0.5 * (grad_up[t] + grad_down[t]) for t in range(2)]
        known = jnp.where(slab == 0, k < K - 2, k > 0)
        open_flux = jnp.where(known, level + 1, FAR) < depth
        down_courant = jnp.where(open_flux, vc[down], 0.0)
        vert = face_flux(down_courant, here, next_row, grad_down, grad_up, grad_far)
        total = []
        for t in range(2):
            total.append(here[t] + below_flux[t] - vert[t])
            below_flux[t] = vert[t]
        rate[k + 1] = jnp.where(level + 1 < depth, jnp.sqrt(tb[k]), 0.0)
        iso_level = jnp.where(k == edge, FAR, level)
        spread = df[k]

        open_west = level < depth_west
        behind = [row_roll(here[t], 1) for t in range(2)]
        grad = [jnp.where(open_west, here[t] - behind[t], 0.0) for t in range(2)]
        flux = face_flux(
            jnp.where(level < depth_west_inner, zc[k], 0.0),
            behind,
            here,
            grad,
            [row_roll(grad[t], 1) for t in range(2)],
            [row_roll(grad[t], -1) for t in range(2)],
        )
        iso = isoneutral(
            grad,
            [0.5 * (centred[t] + row_roll(centred[t], 1)) for t in range(2)],
            jnp.where(iso_level < depth_west_inner, spread, 0.0),
        )
        for t in range(2):
            net = iso[t] - flux[t]
            total[t] = total[t] + (row_roll(net, -1) - net)

        open_south = level < depth_south
        behind = [lane_roll(here[t], 1) for t in range(2)]
        grad = [jnp.where(open_south, here[t] - behind[t], 0.0) for t in range(2)]
        flux = face_flux(
            jnp.where(open_south, mc[k], 0.0),
            behind,
            here,
            grad,
            [lane_roll(grad[t], 1) for t in range(2)],
            [lane_roll(grad[t], -1) for t in range(2)],
        )
        iso = isoneutral(
            grad,
            [0.5 * (centred[t] + lane_roll(centred[t], 1)) for t in range(2)],
            jnp.where(iso_level < depth_south, spread, 0.0),
        )
        for t in range(2):
            net = iso[t] - flux[t]
            total[t] = total[t] + (lane_roll(net, -1) - net)
            for lane in range(LANES):
                p_out[t, lane, pl.ds(k * X, X), :] = total[t][:, lane * 128 : lane * 128 + 128]

    def eliminate(j, tail):
        prev_face = jnp.where(slab == 0, j, K - j)
        next_face = jnp.where(slab == 0, j + 1, K - 1 - j)
        k = jnp.where(slab == 0, j, K - 1 - j)
        prev_rate = rate[prev_face]
        next_rate = rate[next_face]
        rest = 1.0 + prev_rate * tail
        inverse = 1.0 / (rest + next_rate)
        inverse_out[k] = inverse
        carry_out[k] = prev_rate * inverse
        ratio_out[k] = next_rate * inverse
        return rest * inverse

    tail_out[0] = lax.fori_loop(0, K - 1, eliminate, jnp.zeros((X, Y), F32))
    tail_out[1] = rate[jnp.where(slab == 0, K - 1, 1)]


def edge_kernel(
    east_msg, west_msg, level_msg, east_corner, west_corner,
    tracers, zonal, vertical, diffusivity, turbulence, sea, bottom,
    p_in, inverse, carry, tail,
    v_out, meet_out,
    p, cols, zcols, dcols, rows, vrows, drow, trow, sems
):
    slab = lax.axis_index("lev")
    edge = (K - 1) * (1 - slab)
    inner = 30 - 29 * slab
    first = (K - 3) * (1 - slab)
    base = K * slab
    copies = []

    def add(src, dst):
        copies.append(pltpu.make_async_copy(src, dst, sems.at[len(copies)]))

    own = (0, 1, 2, X - 3, X - 2, X - 1)
    for t in range(2):
        for i, x in enumerate(own):
            add(tracers.at[t, x], cols.at[t, i])
        for i in range(3):
            add(tracers.at[t, :, first + i, :], rows.at[t, 2 * slab + i])
    for i, x in enumerate((0, 1, X - 1)):
        add(zonal.at[x], zcols.at[i])
        add(diffusivity.at[x], dcols.at[i])
    add(vertical.at[:, edge, :], vrows.at[0])
    add(vertical.at[:, 1, :], vrows.at[1])
    add(diffusivity.at[:, edge, :], drow)
    add(turbulence.at[:, K - 1, :], trow)
    add(p_in, p)
    run_copies(copies)
    for t in range(2):
        for i in range(2):
            rows[t, 3 * (1 - slab) + i] = level_msg[2 * t + i]

    depth = sea[...] * (bottom[...] + 1)

    level = base + lax.broadcasted_iota(jnp.int32, (K, Y), 0)
    local_row = lax.broadcasted_iota(jnp.int32, (K, Y), 0)

    def zonal_edge(q, depths, halo, courants, spreads):
        centred = []
        for i in range(3):
            column_depth = depths[i + 1]
            pair = []
            for t in range(2):
                mine = q[t][i + 1]
                outer = halo[t][i]
                below = jnp.where(local_row == K - 1, outer, row_roll(mine, -1))
                down = jnp.where(level + 1 < column_depth, below - mine, 0.0)
                top = jnp.where(
                    (slab == 1) & (level < column_depth), mine - outer, 0.0
                )
                up = jnp.where(local_row == 0, top, row_roll(down, 1))
                pair.append(0.5 * (up + down))
            centred.append(pair)
        opened = [level < jnp.minimum(depths[i], depths[i + 1]) for i in range(4)]
        grads = [
            [jnp.where(opened[i], q[t][i + 1] - q[t][i], 0.0) for t in range(2)] for i in range(4)
        ]
        nets = []
        for f in range(2):
            flux = face_flux(
                jnp.where(opened[f + 1], courants[f], 0.0),
                [q[t][f + 1] for t in range(2)],
                [q[t][f + 2] for t in range(2)],
                grads[f + 1],
                grads[f],
                grads[f + 2],
            )
            iso = isoneutral(
                grads[f + 1],
                [0.5 * (centred[f][t] + centred[f + 1][t]) for t in range(2)],
                jnp.where(opened[f + 1], spreads[f], 0.0),
            )
            nets.append([iso[t] - flux[t] for t in range(2)])
        return nets

    def add_column(t, x, values):
        for lane in range(LANES):
            where = (t, lane, pl.ds(x, K, stride=X), slice(None))
            p[where] = p[where] + values[:, lane * 128 : lane * 128 + 128]

    def depth_row(x):
        return depth[x : x + 1]

    def near(t, x):
        return level_msg[2 * t + slab, x : x + 1, :]

    west_depths = east_msg[4 * K : 4 * K + 8, :].astype(jnp.int32)
    nets = zonal_edge(
        [
            [east_msg[(2 * t + i) * K : (2 * t + i + 1) * K, :] for i in range(2)]
            + [cols[t, i] for i in range(3)]
            for t in range(2)
        ],
        [west_depths[6:7], west_depths[7:8], depth_row(0), depth_row(1), depth_row(2)],
        [[east_corner[t : t + 1, :], near(t, 0), near(t, 1)] for t in range(2)],
        [zcols[0], zcols[1]],
        [dcols[0], dcols[1]],
    )
    for t in range(2):
        add_column(t, 0, nets[1][t] - nets[0][t])
        add_column(t, 1, -nets[1][t])
    east_depths = west_msg[6 * K : 6 * K + 8, :].astype(jnp.int32)
    nets = zonal_edge(
        [
            [cols[t, 3 + i] for i in range(3)]
            + [west_msg[(2 * t + i) * K : (2 * t + i + 1) * K, :] for i in range(2)]
            for t in range(2)
        ],
        [depth_row(X - 3), depth_row(X - 2), depth_row(X - 1), east_depths[0:1], east_depths[1:2]],
        [[near(t, X - 2), near(t, X - 1), west_corner[t : t + 1, :]] for t in range(2)],
        [zcols[2], west_msg[4 * K : 5 * K, :]],
        [dcols[2], west_msg[5 * K : 6 * K, :]],
    )
    for t in range(2):
        add_column(t, X - 2, nets[0][t])
        add_column(t, X - 1, nets[1][t] - nets[0][t])

    start = K - 3 + slab
    q = [[rows[t, i] for i in range(5)] for t in range(2)]
    grads = [
        [jnp.where(start + i + 1 < depth, q[t][i + 1] - q[t][i], 0.0) for t in range(2)]
        for i in range(4)
    ]
    other = level_msg[4]
    courant_low = jnp.where(slab == 0, other, vrows[1])
    above = face_flux(
        jnp.where(start + 2 < depth, vrows[0], 0.0),
        [q[t][1] for t in range(2)], [q[t][2] for t in range(2)], grads[1], grads[0], grads[2],
    )
    under = face_flux(
        jnp.where(start + 3 < depth, courant_low, 0.0),
        [q[t][2] for t in range(2)], [q[t][3] for t in range(2)], grads[2], grads[1], grads[3],
    )
    centred = [0.5 * (grads[1][t] + grads[2][t]) for t in range(2)]
    here = [q[t][2] for t in range(2)]
    mid = start + 2
    depth_west = west_depth(depth)
    row = lax.broadcasted_iota(jnp.int32, (X, Y), 0)
    depth_west_inner = jnp.where((row >= 2) & (row <= X - 2), depth_west, 0)
    depth_south = south_depth(depth)
    spread = drow[...]
    grad = [jnp.where(mid < depth_west, here[t] - row_roll(here[t], 1), 0.0) for t in range(2)]
    zonal_iso = isoneutral(
        grad,
        [0.5 * (centred[t] + row_roll(centred[t], 1)) for t in range(2)],
        jnp.where(mid < depth_west_inner, spread, 0.0),
    )
    grad = [jnp.where(mid < depth_south, here[t] - lane_roll(here[t], 1), 0.0) for t in range(2)]
    merid_iso = isoneutral(
        grad,
        [0.5 * (centred[t] + lane_roll(centred[t], 1)) for t in range(2)],
        jnp.where(mid < depth_south, spread, 0.0),
    )

    def add_level(t, k, values):
        for lane in range(LANES):
            where = (t, lane, pl.ds(pl.multiple_of(k * X, X), X), slice(None))
            p[where] = p[where] + values[:, lane * 128 : lane * 128 + 128]

    for t in range(2):
        change = row_roll(zonal_iso[t], -1) - zonal_iso[t]
        change = change + (lane_roll(merid_iso[t], -1) - merid_iso[t])
        add_level(t, edge, change - (under[t] - above[t]))
        add_level(t, inner, jnp.where(slab == 0, -above[t], under[t]))

    def provisional(t, k):
        rows_at = pl.ds(pl.multiple_of(k * X, X), X)
        return jnp.concatenate([p[t, lane, rows_at, :] for lane in range(LANES)], axis=1)

    def forward(j, values):
        k = jnp.where(slab == 0, j, K - 1 - j)
        inv = inverse[k]
        car = carry[k]
        new = tuple(provisional(t, k) * inv + car * values[t] for t in range(2))
        for t in range(2):
            v_out[t, k] = new[t]
        return new

    zero = jnp.zeros((X, Y), F32)
    values = lax.fori_loop(0, K - 1, forward, (zero, zero))
    meet_rate = jnp.where(K < depth, jnp.sqrt(jnp.where(slab == 0, trow[...], other)), 0.0)
    prev_rate = tail[1]
    rest = 1.0 + prev_rate * tail[0]
    inv = 1.0 / (rest + meet_rate)
    for t in range(2):
        meet_out[t] = (provisional(t, edge) + prev_rate * values[t]) * inv
    meet_out[2] = rest * inv


def finish_kernel(v, ratio, mine, theirs, out, u, sems):
    slab = lax.axis_index("lev")
    own_tail = mine[2]
    scale = 1.0 / (own_tail + (1.0 - own_tail) * theirs[2])
    last = tuple((mine[t] + (1.0 - own_tail) * theirs[t]) * scale for t in range(2))
    edge = (K - 1) * (1 - slab)

    def copies(k):
        return [pltpu.make_async_copy(u.at[t, k], out.at[t, :, k, :], sems.at[t, k]) for t in range(2)]

    for t in range(2):
        u[t, edge] = last[t]
    for copy in copies(edge):
        copy.start()

    def backward(i, values):
        j = K - 2 - i
        k = jnp.where(slab == 0, j, K - 1 - j)
        rat = ratio[k]
        new = tuple(v[t, k] + rat * values[t] for t in range(2))
        for t in range(2):
            u[t, k] = new[t]
        for copy in copies(k):
            copy.start()
        return new

    lax.fori_loop(0, K - 1, backward, last)

    @pl.loop(0, K)
    def _(k):
        for copy in copies(k):
            copy.wait()


def shape(*dims):
    return jax.ShapeDtypeStruct(dims, F32)


def params():
    return pltpu.CompilerParams(vmem_limit_bytes=40 * 1024 * 1024)


def local(
    tracers, zonal, merid, vertical, diffusivity, turbulence, sea, bottom
):
    count = lax.axis_size("tile")
    east_msg, west_msg, level_msg, east_corner, west_corner = pl.pallas_call(
        pack_kernel,
        name="pack",
        in_specs=[any_spec()] * 5 + [vmem_spec()] * 2,
        out_specs=[any_spec()] * 5,
        out_shape=[
            shape(4 * K + 8, Y), shape(6 * K + 8, Y), shape(5, X, Y), shape(2, Y), shape(2, Y)
        ],
        scratch_shapes=[pltpu.VMEM((X, Y), F32), pltpu.SemaphoreType.DMA((24,))],
        compiler_params=params(),
    )(tracers, zonal, vertical, diffusivity, turbulence, sea, bottom)

    eastward = [(i, (i + 1) % count) for i in range(count)]
    east_cross = []
    west_cross = []
    for source, target in eastward:
        for slab in range(2):
            east_cross.append((2 * source + slab, 2 * target + 1 - slab))
            west_cross.append((2 * target + slab, 2 * source + 1 - slab))
    east_in = lax.ppermute(east_msg, "tile", eastward)
    west_in = lax.ppermute(west_msg, "tile", [(b, a) for a, b in eastward])
    level_in = lax.ppermute(level_msg, "lev", [(0, 1), (1, 0)])
    east_corner_in = lax.ppermute(east_corner, ("tile", "lev"), east_cross)
    west_corner_in = lax.ppermute(west_corner, ("tile", "lev"), west_cross)

    p, inverse, carry, ratio, tail = pl.pallas_call(
        interior_kernel,
        name="interior",
        in_specs=[any_spec()] * 6 + [vmem_spec()] * 2,
        out_specs=[vmem_spec()] * 5,
        out_shape=[
            shape(2, LANES, K * X, 128), shape(K, X, Y), shape(K, X, Y), shape(K, X, Y), shape(2, X, Y)
        ],
        scratch_shapes=[
            pltpu.VMEM((2, K, X, Y), F32),
            pltpu.VMEM((K, X, Y), F32),
            pltpu.VMEM((K, X, Y), F32),
            pltpu.VMEM((K, X, Y), F32),
            pltpu.VMEM((K, X, Y), F32),
            pltpu.VMEM((K, X, Y), F32),
            pltpu.VMEM((2, X, Y), F32),
            pltpu.VMEM((K + 1, X, Y), F32),
            pltpu.SemaphoreType.DMA((7, K)),
        ],
        compiler_params=params(),
        cost_estimate=pl.CostEstimate(flops=50_000_000, bytes_accessed=40_000_000, transcendentals=0),
    )(tracers, zonal, merid, vertical, diffusivity, turbulence, sea, bottom)

    v, meet = pl.pallas_call(
        edge_kernel,
        name="edges",
        in_specs=[vmem_spec()] * 5 + [any_spec()] * 5 + [vmem_spec()] * 2 + [any_spec()] + [vmem_spec()] * 3,
        out_specs=[vmem_spec()] * 2,
        out_shape=[shape(2, K, X, Y), shape(3, X, Y)],
        scratch_shapes=[
            pltpu.VMEM((2, LANES, K * X, 128), F32),
            pltpu.VMEM((2, 6, K, Y), F32),
            pltpu.VMEM((3, K, Y), F32),
            pltpu.VMEM((3, K, Y), F32),
            pltpu.VMEM((2, 5, X, Y), F32),
            pltpu.VMEM((2, X, Y), F32),
            pltpu.VMEM((X, Y), F32),
            pltpu.VMEM((X, Y), F32),
            pltpu.SemaphoreType.DMA((40,)),
        ],
        compiler_params=params(),
    )(
        east_in, west_in, level_in, east_corner_in, west_corner_in,
        tracers, zonal, vertical, diffusivity, turbulence, sea, bottom,
        p, inverse, carry, tail,
    )

    meet_in = lax.ppermute(meet, "lev", [(0, 1), (1, 0)])
    return pl.pallas_call(
        finish_kernel,
        name="finish",
        in_specs=[vmem_spec()] * 4,
        out_specs=any_spec(),
        out_shape=shape(2, X, K, Y),
        scratch_shapes=[pltpu.VMEM((2, K, X, Y), F32), pltpu.SemaphoreType.DMA((2, K))],
        compiler_params=params(),
    )(v, ratio, meet, meet_in)


def solution(mesh):
    return jax.shard_map(
        local,
        mesh=mesh,
        in_specs=(
            P(None, "tile", "lev", None),
            P("tile", "lev", None),
            P("tile", "lev", None),
            P("tile", "lev", None),
            P("tile", "lev", None),
            P("tile", "lev", None),
            P("tile", None),
            P("tile", None),
        ),
        out_specs=P(None, "tile", "lev", None),
        check_vma=False,
    )
```

profile of v0, /device:TPU:0, one launch (start us, length us, event | category | flops | bytes accessed | tf_op | source)
XLA Modules:
  0.0 54.0 jit_solution(4779674509014629560)
XLA Ops:
  0.0 1.4 %copy-done = f32[2,16,32,384]{3,2,1,0:T(8,128)S(1)} copy-done((f32[2,16,32,384]{3,2,1,0:T(8,128)S(1)}, f32[2,16,32,384]{3,2,1,0:T(8,128)}, u32[]{:S(2)}) %copy-start) | copy-done | bytes 1572888
  1.4 1.1 %copy-done.1 = f32[16,32,384]{2,1,0:T(8,128)S(1)} copy-done((f32[16,32,384]{2,1,0:T(8,128)S(1)}, f32[16,32,384]{2,1,0:T(8,128)}, u32[]{:S(2)}) %copy-start.1) | copy-done | bytes 786456
  2.5 1.1 %copy-done.2 = f32[16,32,384]{2,1,0:T(8,128)S(1)} copy-done((f32[16,32,384]{2,1,0:T(8,128)S(1)}, f32[16,32,384]{2,1,0:T(8,128)}, u32[]{:S(2)}) %copy-start.2) | copy-done | bytes 786456
  3.7 1.1 %copy-done.3 = f32[16,32,384]{2,1,0:T(8,128)S(1)} copy-done((f32[16,32,384]{2,1,0:T(8,128)S(1)}, f32[16,32,384]{2,1,0:T(8,128)}, u32[]{:S(2)}) %copy-start.3) | copy-done | bytes 786456
  4.8 1.1 %copy-done.4 = f32[16,32,384]{2,1,0:T(8,128)S(1)} copy-done((f32[16,32,384]{2,1,0:T(8,128)S(1)}, f32[16,32,384]{2,1,0:T(8,128)}, u32[]{:S(2)}) %copy-start.4) | copy-done | bytes 786456
  5.9 0.7 %copy-done.6 = s32[16,384]{1,0:T(8,128)S(1)} copy-done((s32[16,384]{1,0:T(8,128)S(1)}, s32[16,384]{1,0:T(8,128)}, u32[]{:S(2)}) %copy-start.6) | copy-done | bytes 24600
  6.7 0.7 %copy-done.7 = s32[16,384]{1,0:T(8,128)S(1)} copy-done((s32[16,384]{1,0:T(8,128)S(1)}, s32[16,384]{1,0:T(8,128)}, u32[]{:S(2)}) %copy-start.7) | copy-done | bytes 24600
  7.4 1.0 %pack.1 = (f32[136,384]{1,0:T(8,128)S(1)}, f32[200,384]{1,0:T(8,128)S(1)}, f32[5,16,384]{2,1,0:T(8,128)S(1)}, f32[2,384]{1,0:T(2,128)S(1)}, f32[2,384]{1,0:T(2,128)S(1)}) custom-call(f32[2,16,32,384]{3,2,1,0:T(8,128)S(1)} %copy-done, f32[16,32,384]{2,1,0:T(8,128)S(1)} %copy-done.1, f32[16,32,384]{2,1,0:T(8,128)S(1)} %copy-done.2, ...), custom_call_target="tpu_custom_call" | custom-call | tf_op jit(solution)/shard_map/pack/pallas_call | solution.py:495
  8.5 7.0 %collective-permute-start.1 = (f32[200,384]{1,0:T(8,128)S(1)}, f32[200,384]{1,0:T(8,128)S(1)}, u32[]{:S(2)}, u32[]{:S(2)}) collective-permute-start(f32[200,384]{1,0:T(8,128)S(1)} %get-tuple-element.18), channel_id=1, source_target_pairs={{2,0},{4,2},{6,4},{8,6},{10,8},{12,10},{14,12},{16,14},{18,16},{20... | collective-permute-start | bytes 921608 | tf_op jit(solution)/shard_map/ppermute | solution.py:515
  15.5 0.0 collective-permute-start
  15.5 2.7 %collective-permute-start.2 = (f32[5,16,384]{2,1,0:T(8,128)S(1)}, f32[5,16,384]{2,1,0:T(8,128)S(1)}, u32[]{:S(2)}, u32[]{:S(2)}) collective-permute-start(f32[5,16,384]{2,1,0:T(8,128)S(1)} %get-tuple-element.19), channel_id=1, source_target_pairs={{0,1},{1,0},{2,3},{3,2},{4,5},{5,4},{6,7},{7,6},{8,9},{9,8},{10,11... | collective-permute-start | bytes 368648 | tf_op jit(solution)/shard_map/ppermute | solution.py:516
  18.2 0.0 collective-permute-start.3
  18.2 7.2 %collective-permute-start.4 = (f32[2,384]{1,0:T(2,128)S(1)}, f32[2,384]{1,0:T(2,128)S(1)}, u32[]{:S(2)}, u32[]{:S(2)}) collective-permute-start(f32[2,384]{1,0:T(2,128)S(1)} %get-tuple-element.21), channel_id=1, source_target_pairs={{2,1},{3,0},{4,3},{5,2},{6,5},{7,4},{8,7},{9,6},{10,9},{11,8},{12,... | collective-permute-start | bytes 9224 | tf_op jit(solution)/shard_map/ppermute | solution.py:518
  25.4 0.0 copy-done.5
  25.4 16.8 %interior.1 = (f32[2,3,512,128]{3,2,1,0:T(8,128)S(1)}, f32[32,16,384]{2,1,0:T(8,128)S(1)}, f32[32,16,384]{2,1,0:T(8,128)S(1)}, f32[32,16,384]{2,1,0:T(8,128)S(1)}, f32[2,16,384]{2,1,0:T(8,128)S(1)}) custom-call(f32[2,16,32,384]{3,2,1,0:T(8,128)S(1)} %copy-done, f32[16,32,384]{2,1,0:T(8,128)S(1)} %copy-done.1, f32[16,32,384]{2,1,0:T(8,128)S(1)} %copy-done.5, ...), custom_call_target="tpu_custom_call" | custom-call | flops 50000000 | bytes 40000000 | tf_op jit(solution)/shard_map/interior/pallas_call | solution.py:520
  42.2 0.0 collective-permute-done.3.east_corner
  42.2 0.0 collective-permute-done.4.west_corner
  42.3 0.0 collective-permute-done.2.level_msg
  42.3 0.0 collective-permute-done.east_msg
  42.3 0.0 collective-permute-done.1.west_msg
  42.3 3.7 %edges.1 = (f32[2,32,16,384]{3,2,1,0:T(8,128)S(1)}, f32[3,16,384]{2,1,0:T(8,128)S(1)}) custom-call(f32[136,384]{1,0:T(8,128)S(1)} %collective-permute-done.east_msg, f32[200,384]{1,0:T(8,128)S(1)} %collective-permute-done.1.west_msg, f32[5,16,384]{2,1,0:T(8,128)S(1)} %collective-permute-done.2.level_msg, f32[2,384]{1,0:T(2,128)S(1)} %collective-permute-done.3.east_corner, ...), custom_call_target="tpu_custom_call" | custom-call | tf_op jit(solution)/shard_map/edges/pallas_call | solution.py:543
  46.0 0.1 collective-permute-start.5
  46.1 5.8 %collective-permute-done.5.theirs = f32[3,16,384]{2,1,0:T(8,128)S(1)} collective-permute-done((f32[3,16,384]{2,1,0:T(8,128)S(1)}, f32[3,16,384]{2,1,0:T(8,128)S(1)}, u32[]{:S(2)}, u32[]{:S(2)}) %collective-permute-start.5) | collective-permute-done | bytes 73760 | tf_op jit(solution)/shard_map/ppermute | solution.py:567
  52.0 2.0 %finish.1 = f32[2,16,32,384]{3,2,1,0:T(8,128)} custom-call(f32[2,32,16,384]{3,2,1,0:T(8,128)S(1)} %get-tuple-element.26.v, f32[32,16,384]{2,1,0:T(8,128)S(1)} %get-tuple-element.27.ratio, f32[3,16,384]{2,1,0:T(8,128)S(1)} %get-tuple-element.28.mine, f32[3,16,384]{2,1,0:T(8,128)S(1)} %collective-permute-done.5.theirs), custom_call_target="tpu_custom_call" | custom-call | tf_op jit(solution)/shard_map/finish/pallas_call | solution.py:568
  (8 shorter events, 0.0 us)
Async XLA Ops:
  0.0 1.4 %copy-start = (f32[2,16,32,384]{3,2,1,0:T(8,128)S(1)}, f32[2,16,32,384]{3,2,1,0:T(8,128)}, u32[]{:S(2)}) copy-start(f32[2,16,32,384]{3,2,1,0:T(8,128)} %tracers.5) | copy-start | bytes 4718596
  1.4 1.1 %copy-start.1 = (f32[16,32,384]{2,1,0:T(8,128)S(1)}, f32[16,32,384]{2,1,0:T(8,128)}, u32[]{:S(2)}) copy-start(f32[16,32,384]{2,1,0:T(8,128)} %zonal.5) | copy-start | bytes 2359300
  2.5 1.1 %copy-start.2 = (f32[16,32,384]{2,1,0:T(8,128)S(1)}, f32[16,32,384]{2,1,0:T(8,128)}, u32[]{:S(2)}) copy-start(f32[16,32,384]{2,1,0:T(8,128)} %vertical.5) | copy-start | bytes 2359300
  3.7 1.1 %copy-start.3 = (f32[16,32,384]{2,1,0:T(8,128)S(1)}, f32[16,32,384]{2,1,0:T(8,128)}, u32[]{:S(2)}) copy-start(f32[16,32,384]{2,1,0:T(8,128)} %diffusivity.5) | copy-start | bytes 2359300
  4.8 1.1 %copy-start.4 = (f32[16,32,384]{2,1,0:T(8,128)S(1)}, f32[16,32,384]{2,1,0:T(8,128)}, u32[]{:S(2)}) copy-start(f32[16,32,384]{2,1,0:T(8,128)} %turbulence.5) | copy-start | bytes 2359300
  5.9 0.7 %copy-start.6 = (s32[16,384]{1,0:T(8,128)S(1)}, s32[16,384]{1,0:T(8,128)}, u32[]{:S(2)}) copy-start(s32[16,384]{1,0:T(8,128)} %sea.5) | copy-start | bytes 73732
  6.7 0.7 %copy-start.7 = (s32[16,384]{1,0:T(8,128)S(1)}, s32[16,384]{1,0:T(8,128)}, u32[]{:S(2)}) copy-start(s32[16,384]{1,0:T(8,128)} %bottom.5) | copy-start | bytes 73732
  7.4 18.0 %copy-start.5 = (f32[16,32,384]{2,1,0:T(8,128)S(1)}, f32[16,32,384]{2,1,0:T(8,128)}, u32[]{:S(2)}) copy-start(f32[16,32,384]{2,1,0:T(8,128)} %merid.1) | copy-start | bytes 2359300
  8.5 33.8 %collective-permute-start.1 = (f32[200,384]{1,0:T(8,128)S(1)}, f32[200,384]{1,0:T(8,128)S(1)}, u32[]{:S(2)}, u32[]{:S(2)}) collective-permute-start(f32[200,384]{1,0:T(8,128)S(1)} %get-tuple-element.18), channel_id=1, source_target_pairs={{2,0},{4,2},{6,4},{8,6},{10,8},{12,10},{14,12},{16,14},{18,16},{20... | collective-permute-start | bytes 921608 | tf_op jit(solution)/shard_map/ppermute | solution.py:515
  15.5 26.8 %collective-permute-start = (f32[136,384]{1,0:T(8,128)S(1)}, f32[136,384]{1,0:T(8,128)S(1)}, u32[]{:S(2)}, u32[]{:S(2)}) collective-permute-start(f32[136,384]{1,0:T(8,128)S(1)} %get-tuple-element.17), channel_id=1, source_target_pairs={{0,2},{2,4},{4,6},{6,8},{8,10},{10,12},{12,14},{14,16},{16,18},{18... | collective-permute-start | bytes 626696 | tf_op jit(solution)/shard_map/ppermute | solution.py:514
  15.5 26.8 %collective-permute-start.2 = (f32[5,16,384]{2,1,0:T(8,128)S(1)}, f32[5,16,384]{2,1,0:T(8,128)S(1)}, u32[]{:S(2)}, u32[]{:S(2)}) collective-permute-start(f32[5,16,384]{2,1,0:T(8,128)S(1)} %get-tuple-element.19), channel_id=1, source_target_pairs={{0,1},{1,0},{2,3},{3,2},{4,5},{5,4},{6,7},{7,6},{8,9},{9,8},{10,11... | collective-permute-start | bytes 368648 | tf_op jit(solution)/shard_map/ppermute | solution.py:516
  18.2 24.0 %collective-permute-start.3 = (f32[2,384]{1,0:T(2,128)S(1)}, f32[2,384]{1,0:T(2,128)S(1)}, u32[]{:S(2)}, u32[]{:S(2)}) collective-permute-start(f32[2,384]{1,0:T(2,128)S(1)} %get-tuple-element.20), channel_id=1, source_target_pairs={{0,3},{1,2},{2,5},{3,4},{4,7},{5,6},{6,9},{7,8},{8,11},{9,10},{10,... | collective-permute-start | bytes 9224 | tf_op jit(solution)/shard_map/ppermute | solution.py:517
  18.2 24.0 %collective-permute-start.4 = (f32[2,384]{1,0:T(2,128)S(1)}, f32[2,384]{1,0:T(2,128)S(1)}, u32[]{:S(2)}, u32[]{:S(2)}) collective-permute-start(f32[2,384]{1,0:T(2,128)S(1)} %get-tuple-element.21), channel_id=1, source_target_pairs={{2,1},{3,0},{4,3},{5,2},{6,5},{7,4},{8,7},{9,6},{10,9},{11,8},{12,... | collective-permute-start | bytes 9224 | tf_op jit(solution)/shard_map/ppermute | solution.py:518
  46.0 5.9 %collective-permute-start.5 = (f32[3,16,384]{2,1,0:T(8,128)S(1)}, f32[3,16,384]{2,1,0:T(8,128)S(1)}, u32[]{:S(2)}, u32[]{:S(2)}) collective-permute-start(f32[3,16,384]{2,1,0:T(8,128)S(1)} %get-tuple-element.28.mine), channel_id=1, source_target_pairs={{0,1},{1,0},{2,3},{3,2},{4,5},{5,4},{6,7},{7,6},{8,9},{9,8},{10,11... | collective-permute-start | bytes 221192 | tf_op jit(solution)/shard_map/ppermute | solution.py:567
where the time goes:
time: 54.4 us; the launch traced here: 54 us
  Pallas kernels  23.6 us (43%)
  starting transfers between devices  17 us (31%)
  local copies, waits for them, and re-layouts  7.42 us (14%)
  waiting for transfers between devices  5.86 us (11%)
    pallas_call x1, Pallas kernels, local(): pl.pallas_call(interior_kernel, name='interior', in_specs=[any_spec()] *...  16.8 us
    unnamed x16, local copies, waits for them, and re-layouts  7.42 us
    ppermute x1, starting transfers between devices, local(): west_corner_in = lax.ppermute(west_corner, ('tile', 'lev'), west_cross)  7.17 us
    ppermute x1, starting transfers between devices, local(): west_in = lax.ppermute(west_msg, 'tile', [(b, a) for a, b in eastward])  7.01 us
    ppermute x1, waiting for transfers between devices, local(): meet_in = lax.ppermute(meet, 'lev', [(0, 1), (1, 0)])  5.84 us
    pallas_call x1, Pallas kernels, local(): pl.pallas_call(edge_kernel, name='edges', in_specs=[vmem_spec()] * 5 + [a...  3.74 us
    ppermute x1, starting transfers between devices, local(): level_in = lax.ppermute(level_msg, 'lev', [(0, 1), (1, 0)])  2.73 us
    pallas_call x1, Pallas kernels, local(): pl.pallas_call(finish_kernel, name='finish', in_specs=[vmem_spec()] * 4,...  1.98 us
  transfers between devices with their start and end apart: 6, of which 1 were waited for; matrix products, arithmetic and copies ran while one was open for 0% of the time, Pallas kernels for 31%

commit v1 on v0

v1 whole, which is shorter than its diff:
```python
import jax
import jax.numpy as jnp
from jax import lax
from jax.experimental import pallas as pl
from jax.experimental.pallas import tpu as pltpu
from jax.sharding import PartitionSpec as P

thermal_coef = 0.2
haline_coef = 0.8
taper_eps = 0.05

X = 16
K = 32
Y = 384
LANES = 3
UNROLL = 2
AHEAD = 8
FAR = 1 << 20
F32 = jnp.float32


def any_spec():
    return pl.BlockSpec(memory_space=pl.ANY)


def vmem_spec():
    return pl.BlockSpec(memory_space=pltpu.VMEM)


def face_flux(courant, behind, grad, back, front):
    half = 0.5 * courant
    half_speed = jnp.abs(half)
    weight = half_speed - 2.0 * half_speed * half_speed
    lag = half - half_speed
    forward = courant > 0.0
    fluxes = []
    for t in range(2):
        upwind = jnp.where(forward, back[t], front[t])
        low = jnp.minimum(grad[t], 0.0)
        high = jnp.maximum(grad[t], 0.0)
        double = jnp.minimum(jnp.maximum(upwind + upwind, low), high)
        excess = jnp.minimum(jnp.maximum(upwind - grad[t], low), high)
        fluxes.append(courant * behind[t] + lag * grad[t] + weight * (double + excess))
    return fluxes


def reciprocal(values):
    guess = pl.reciprocal(values, approx=True)
    return guess * (2.0 - values * guess)


def isoneutral(grad, vert, coeff):
    ratio = haline_coef / thermal_coef
    dens_side = ratio * grad[1] - grad[0]
    dens_vert = ratio * vert[1] - vert[0]
    floor = 16.0 * taper_eps / (thermal_coef * thermal_coef)
    slope = dens_side * dens_vert * reciprocal(dens_vert * dens_vert + floor)
    return [coeff * (grad[t] - slope * vert[t]) for t in range(2)]


def lane_roll(values, shift):
    return pltpu.roll(values, shift % Y, 1)


def row_roll(values, shift):
    return pltpu.roll(values, shift % values.shape[0], 0)


def south_depth(depth):
    lane = lax.broadcasted_iota(jnp.int32, depth.shape, 1)
    return jnp.where(lane == 0, 0, jnp.minimum(depth, lane_roll(depth, 1)))


def west_depth(depth):
    return jnp.minimum(depth, row_roll(depth, 1))


def pack_kernel(
    tracers, zonal, vertical, diffusivity, turbulence, sea, bottom,
    east_msg, west_msg, level_msg, depth_rows, sems
):
    slab = lax.axis_index("lev")
    first = (K - 2) * (1 - slab)
    copies = []

    def add(src, dst):
        copies.append(pltpu.make_async_copy(src, dst, sems.at[len(copies)]))
        copies[-1].start()

    for t in range(2):
        for i in range(2):
            rows = pl.ds((2 * t + i) * K, K)
            add(tracers.at[t, X - 2 + i], east_msg.at[rows])
            add(tracers.at[t, i], west_msg.at[rows])
            add(tracers.at[t, :, first + i, :], level_msg.at[2 * t + i])
    add(zonal.at[0], west_msg.at[pl.ds(4 * K, K)])
    add(diffusivity.at[0], west_msg.at[pl.ds(5 * K, K)])
    fifth = len(copies)
    upper = pltpu.make_async_copy(turbulence.at[:, K - 1, :], level_msg.at[4], sems.at[fifth])
    lower = pltpu.make_async_copy(vertical.at[:, 0, :], level_msg.at[4], sems.at[fifth])

    @pl.when(slab == 0)
    def _():
        upper.start()

    @pl.when(slab == 1)
    def _():
        lower.start()

    depth_rows[...] = (sea[...] * (bottom[...] + 1)).astype(F32)
    last = [
        pltpu.make_async_copy(depth_rows.at[pl.ds(8, 8)], east_msg.at[pl.ds(4 * K, 8)], sems.at[fifth + 1]),
        pltpu.make_async_copy(depth_rows.at[pl.ds(0, 8)], west_msg.at[pl.ds(6 * K, 8)], sems.at[fifth + 2]),
    ]
    for copy in last:
        copy.start()
    upper.wait()
    for copy in copies + last:
        copy.wait()


def interior_kernel(
    tracers, zonal, merid, vertical, diffusivity, turbulence, sea, bottom,
    p_out, inverse_out, carry_out, ratio_out, tail_out, cols, zcols, dcols, own_rows, extra_rows,
    q, zc, mc, vc, df, tb, below_flux, rate, sems, col_sems
):
    slab = lax.axis_index("lev")
    edge = (K - 1) * (1 - slab)
    base = K * slab

    def copies(k):
        pairs = [
            (tracers.at[:, :, k, :], q.at[:, k]),
            (zonal.at[:, k, :], zc.at[k]),
            (merid.at[:, k, :], mc.at[k]),
            (vertical.at[:, k, :], vc.at[k]),
            (diffusivity.at[:, k, :], df.at[k]),
            (turbulence.at[:, k, :], tb.at[k]),
        ]
        return [pltpu.make_async_copy(a, b, sems.at[i, k]) for i, (a, b) in enumerate(pairs)]

    for k in range(AHEAD):
        for copy in copies(k):
            copy.start()

    depth = sea[...] * (bottom[...] + 1)
    depth_west = west_depth(depth)
    row = lax.broadcasted_iota(jnp.int32, (X, Y), 0)
    depth_west_inner = jnp.where((row >= 2) & (row <= X - 2), depth_west, 0)
    depth_south = south_depth(depth)
    column_copies = []

    def add(src, dst):
        column_copies.append(pltpu.make_async_copy(src, dst, col_sems.at[len(column_copies)]))
        column_copies[-1].start()

    for i, x in enumerate((0, 1, 2, X - 3, X - 2, X - 1)):
        for t in range(2):
            add(tracers.at[t, x], cols.at[t, i])
    for i, x in enumerate((0, 1, X - 1)):
        add(zonal.at[x], zcols.at[i])
        add(diffusivity.at[x], dcols.at[i])
    below_flux[...] = jnp.zeros_like(below_flux)
    rate[0] = jnp.zeros((X, Y), F32)

    for k in range(2):
        for copy in copies(k):
            copy.wait()

    def process(k, below):
        ahead = jnp.minimum(k + 2, K - 1)
        level = base + k
        up = jnp.maximum(k - 1, 0)
        down = jnp.minimum(k + 1, K - 1)
        here = [q[t, k] for t in range(2)]
        next_row = [q[t, down] for t in range(2)]
        open_up = jnp.where(k > 0, level, FAR) < depth
        open_down = jnp.where(k < K - 1, level + 1, FAR) < depth
        open_far = jnp.where(k < K - 2, level + 2, FAR) < depth
        grad_up = [jnp.where(open_up, here[t] - q[t, up], 0.0) for t in range(2)]
        grad_down = [jnp.where(open_down, next_row[t] - here[t], 0.0) for t in range(2)]
        grad_far = [jnp.where(open_far, q[t, ahead] - next_row[t], 0.0) for t in range(2)]
        centred = [grad_up[t] + grad_down[t] for t in range(2)]
        known = jnp.where(slab == 0, k < K - 2, k > 0)
        open_flux = jnp.where(known, level + 1, FAR) < depth
        down_courant = jnp.where(open_flux, vc[down], 0.0)
        vert = face_flux(down_courant, here, grad_down, grad_up, grad_far)
        total = []
        for t in range(2):
            total.append(here[t] + below[t] - vert[t])
        rate[k + 1] = jnp.where(level + 1 < depth, tb[k] * lax.rsqrt(tb[k]), 0.0)
        iso_level = jnp.where(k == edge, FAR, level)
        spread = df[k]

        open_west = level < depth_west
        behind = [row_roll(here[t], 1) for t in range(2)]
        grad = [jnp.where(open_west, here[t] - behind[t], 0.0) for t in range(2)]
        flux = face_flux(
            jnp.where(level < depth_west_inner, zc[k], 0.0),
            behind,
            grad,
            [row_roll(grad[t], 1) for t in range(2)],
            [row_roll(grad[t], -1) for t in range(2)],
        )
        iso = isoneutral(
            grad,
            [centred[t] + row_roll(centred[t], 1) for t in range(2)],
            jnp.where(iso_level < depth_west_inner, spread, 0.0),
        )
        for t in range(2):
            net = iso[t] - flux[t]
            total[t] = total[t] + (row_roll(net, -1) - net)

        open_south = level < depth_south
        behind = [lane_roll(here[t], 1) for t in range(2)]
        grad = [jnp.where(open_south, here[t] - behind[t], 0.0) for t in range(2)]
        flux = face_flux(
            jnp.where(open_south, mc[k], 0.0),
            behind,
            grad,
            [lane_roll(grad[t], 1) for t in range(2)],
            [lane_roll(grad[t], -1) for t in range(2)],
        )
        iso = isoneutral(
            grad,
            [centred[t] + lane_roll(centred[t], 1) for t in range(2)],
            jnp.where(iso_level < depth_south, spread, 0.0),
        )
        for t in range(2):
            net = iso[t] - flux[t]
            total[t] = total[t] + (lane_roll(net, -1) - net)
            for lane in range(LANES):
                p_out[t, lane, pl.ds(k * X, X), :] = total[t][:, lane * 128 : lane * 128 + 128]
        return vert

    @pl.loop(0, K // UNROLL)
    def _(i):
        first = i * UNROLL
        for u in range(UNROLL):
            @pl.when(first + u + AHEAD < K)
            def _():
                for copy in copies(first + u + AHEAD):
                    copy.start()

            @pl.when(first + u + 2 < K)
            def _():
                for copy in copies(first + u + 2):
                    copy.wait()

        below = [below_flux[t] for t in range(2)]
        for u in range(UNROLL):
            below = process(first + u, below)
        for t in range(2):
            below_flux[t] = below[t]

    def eliminate(j, tail):
        prev_face = jnp.where(slab == 0, j, K - j)
        next_face = jnp.where(slab == 0, j + 1, K - 1 - j)
        k = jnp.where(slab == 0, j, K - 1 - j)
        prev_rate = rate[prev_face]
        next_rate = rate[next_face]
        rest = 1.0 + prev_rate * tail
        inverse = reciprocal(rest + next_rate)
        inverse_out[k] = inverse
        carry_out[k] = prev_rate * inverse
        ratio_out[k] = next_rate * inverse
        return rest * inverse

    tail_out[0] = lax.fori_loop(0, K - 1, eliminate, jnp.zeros((X, Y), F32))
    tail_out[1] = rate[jnp.where(slab == 0, K - 1, 1)]
    for t in range(2):
        for i in range(3):
            own_rows[t, i] = q[t, (K - 3) * (1 - slab) + i]
    extra_rows[0] = vc[edge]
    extra_rows[1] = vc[1]
    extra_rows[2] = df[edge]
    extra_rows[3] = tb[K - 1]
    for copy in column_copies:
        copy.wait()


def edge_kernel(
    east_msg, west_msg, level_msg, sea, bottom,
    p_in, inverse, carry, tail, cols, zcols, dcols, own_rows, extra_rows,
    v_out, meet_out, corner_out,
    p, rows, sem
):
    slab = lax.axis_index("lev")
    edge = (K - 1) * (1 - slab)
    inner = 30 - 29 * slab
    base = K * slab
    fetch = pltpu.make_async_copy(p_in, p, sem)
    fetch.start()
    for t in range(2):
        for i in range(3):
            rows[t, 2 * slab + i] = own_rows[t, i]
        for i in range(2):
            rows[t, 3 * (1 - slab) + i] = level_msg[2 * t + i]

    depth = sea[...] * (bottom[...] + 1)

    level = base + lax.broadcasted_iota(jnp.int32, (K, Y), 0)
    local_row = lax.broadcasted_iota(jnp.int32, (K, Y), 0)

    def zonal_edge(q, depths, halo, courants, spreads, outer_face):
        centred = []
        for i in range(3):
            column_depth = depths[i + 1]
            pair = []
            for t in range(2):
                mine = q[t][i + 1]
                outer = halo[t][i]
                below = jnp.where(local_row == K - 1, outer, row_roll(mine, -1))
                down = jnp.where(level + 1 < column_depth, below - mine, 0.0)
                top = jnp.where(
                    (slab == 1) & (level < column_depth), mine - outer, 0.0
                )
                up = jnp.where(local_row == 0, top, row_roll(down, 1))
                pair.append(up + down)
            centred.append(pair)
        opened = [level < jnp.minimum(depths[i], depths[i + 1]) for i in range(4)]
        grads = [
            [jnp.where(opened[i], q[t][i + 1] - q[t][i], 0.0) for t in range(2)] for i in range(4)
        ]
        nets = []
        for f in range(2):
            flux = face_flux(
                jnp.where(opened[f + 1], courants[f], 0.0),
                [q[t][f + 1] for t in range(2)],
                grads[f + 1],
                grads[f],
                grads[f + 2],
            )
            iso = isoneutral(
                grads[f + 1],
                [centred[f][t] + centred[f + 1][t] for t in range(2)],
                jnp.where(opened[f + 1] & (local_row != edge) if f == outer_face else opened[f + 1], spreads[f], 0.0),
            )
            nets.append([iso[t] - flux[t] for t in range(2)])
        return nets

    def add_column(t, x, values):
        for lane in range(LANES):
            where = (t, lane, pl.ds(x, K, stride=X), slice(None))
            p[where] = p[where] + values[:, lane * 128 : lane * 128 + 128]

    def depth_row(x):
        return depth[x : x + 1]

    def near(t, x):
        return level_msg[2 * t + slab, x : x + 1, :]

    west_depths = east_msg[4 * K : 4 * K + 8, :].astype(jnp.int32)
    nets = zonal_edge(
        [
            [east_msg[(2 * t + i) * K : (2 * t + i + 1) * K, :] for i in range(2)]
            + [cols[t, i] for i in range(3)]
            for t in range(2)
        ],
        [west_depths[6:7], west_depths[7:8], depth_row(0), depth_row(1), depth_row(2)],
        [[near(t, 0), near(t, 0), near(t, 1)] for t in range(2)],
        [zcols[0], zcols[1]],
        [dcols[0], dcols[1]],
        0,
    )
    fetch.wait()
    for t in range(2):
        add_column(t, 0, nets[1][t] - nets[0][t])
        add_column(t, 1, -nets[1][t])
    east_depths = west_msg[6 * K : 6 * K + 8, :].astype(jnp.int32)
    nets = zonal_edge(
        [
            [cols[t, 3 + i] for i in range(3)]
            + [west_msg[(2 * t + i) * K : (2 * t + i + 1) * K, :] for i in range(2)]
            for t in range(2)
        ],
        [depth_row(X - 3), depth_row(X - 2), depth_row(X - 1), east_depths[0:1], east_depths[1:2]],
        [[near(t, X - 2), near(t, X - 1), near(t, X - 1)] for t in range(2)],
        [zcols[2], west_msg[4 * K : 5 * K, :]],
        [dcols[2], west_msg[5 * K : 6 * K, :]],
        1,
    )
    for t in range(2):
        add_column(t, X - 2, nets[0][t])
        add_column(t, X - 1, nets[1][t] - nets[0][t])

    start = K - 3 + slab
    q = [[rows[t, i] for i in range(5)] for t in range(2)]
    grads = [
        [jnp.where(start + i + 1 < depth, q[t][i + 1] - q[t][i], 0.0) for t in range(2)]
        for i in range(4)
    ]
    other = level_msg[4]
    courant_low = jnp.where(slab == 0, other, extra_rows[1])
    above = face_flux(
        jnp.where(start + 2 < depth, extra_rows[0], 0.0),
        [q[t][1] for t in range(2)], grads[1], grads[0], grads[2],
    )
    under = face_flux(
        jnp.where(start + 3 < depth, courant_low, 0.0),
        [q[t][2] for t in range(2)], grads[2], grads[1], grads[3],
    )
    centred = [grads[1][t] + grads[2][t] for t in range(2)]
    here = [q[t][2] for t in range(2)]
    mid = start + 2
    depth_west = west_depth(depth)
    row = lax.broadcasted_iota(jnp.int32, (X, Y), 0)
    depth_west_inner = jnp.where((row >= 2) & (row <= X - 2), depth_west, 0)
    depth_south = south_depth(depth)
    spread = extra_rows[2]
    grad = [jnp.where(mid < depth_west, here[t] - row_roll(here[t], 1), 0.0) for t in range(2)]
    zonal_iso = isoneutral(
        grad,
        [centred[t] + row_roll(centred[t], 1) for t in range(2)],
        jnp.where(mid < depth_west_inner, spread, 0.0),
    )
    grad = [jnp.where(mid < depth_south, here[t] - lane_roll(here[t], 1), 0.0) for t in range(2)]
    merid_iso = isoneutral(
        grad,
        [centred[t] + lane_roll(centred[t], 1) for t in range(2)],
        jnp.where(mid < depth_south, spread, 0.0),
    )

    def add_level(t, k, values):
        for lane in range(LANES):
            where = (t, lane, pl.ds(pl.multiple_of(k * X, X), X), slice(None))
            p[where] = p[where] + values[:, lane * 128 : lane * 128 + 128]

    for t in range(2):
        change = row_roll(zonal_iso[t], -1) - zonal_iso[t]
        change = change + (lane_roll(merid_iso[t], -1) - merid_iso[t])
        add_level(t, edge, change - (under[t] - above[t]))
        add_level(t, inner, jnp.where(slab == 0, -above[t], under[t]))

    def provisional(t, k):
        rows_at = pl.ds(pl.multiple_of(k * X, X), X)
        return jnp.concatenate([p[t, lane, rows_at, :] for lane in range(LANES)], axis=1)

    def forward(j, values):
        k = jnp.where(slab == 0, j, K - 1 - j)
        inv = inverse[k]
        car = carry[k]
        new = tuple(provisional(t, k) * inv + car * values[t] for t in range(2))
        for t in range(2):
            v_out[t, k] = new[t]
        return new

    zero = jnp.zeros((X, Y), F32)
    values = lax.fori_loop(0, K - 1, forward, (zero, zero))
    meet_rate = jnp.where(K < depth, jnp.sqrt(jnp.where(slab == 0, extra_rows[3], other)), 0.0)
    prev_rate = tail[1]
    rest = 1.0 + prev_rate * tail[0]
    inv = 1.0 / (rest + meet_rate)
    for t in range(2):
        meet_out[t] = (provisional(t, edge) + prev_rate * values[t]) * inv
    meet_out[2] = rest * inv

    corner_out[...] = jnp.zeros_like(corner_out)
    meet_out[3] = jnp.zeros((X, Y), F32)
    own_level = base + edge
    outside = ((east_msg, K, west_depths[7:8], 0), (west_msg, 0, east_depths[0:1], X - 1))
    open_inner = jnp.where(slab == 0, K - 1, K + 1)
    open_other = jnp.where(slab == 0, K + 1, K - 1)
    for side, (msg, offset, outer_depth, x) in enumerate(outside):
        column_depth = depth_row(x)
        for t in range(2):
            at_edge = offset + 2 * t * K + edge
            outer = msg[pl.ds(at_edge, 1), :]
            outer_inner = msg[pl.ds(offset + 2 * t * K + inner, 1), :]
            meet_out[3, 2 * t + side : 2 * t + side + 1, :] = outer
            meet_out[3, 4 + 2 * t + side : 5 + 2 * t + side, :] = jnp.where(
                open_inner < outer_depth, outer - outer_inner, 0.0
            )
            mine = own_rows[t, 2 * (1 - slab), x : x + 1, :]
            mine_inner = own_rows[t, 1, x : x + 1, :]
            theirs = near(t, x)
            theirs_inner = level_msg[2 * t + 1 - slab, x : x + 1, :]
            cross = jnp.where(K < column_depth, theirs - mine, 0.0)
            corner_out[t, side : side + 1, :] = mine
            corner_out[t, 2 + side : 3 + side, :] = theirs
            corner_out[2 + t, side : side + 1, :] = cross + jnp.where(
                open_inner < column_depth, mine - mine_inner, 0.0
            )
            corner_out[2 + t, 2 + side : 3 + side, :] = (
                jnp.where(open_other < column_depth, theirs - theirs_inner, 0.0) - cross
            )
        spread_row = dcols[0, pl.ds(edge, 1), :] if side == 0 else west_msg[pl.ds(5 * K + edge, 1), :]
        meet_out[3, 8 + side : 9 + side, :] = jnp.where(
            own_level < jnp.minimum(outer_depth, column_depth), spread_row, 0.0
        )
        meet_out[3, 10 + side : 11 + side, :] = inv[x : x + 1]
        shared = jnp.where(K < outer_depth, 1.0, 0.0)
        corner_out[4, side : side + 1, :] = shared
        corner_out[4, 2 + side : 3 + side, :] = shared


def finish_kernel(v, ratio, mine, theirs, corner, out, u, gathered, change, sems):
    slab = lax.axis_index("lev")
    for i in range(6):
        gathered[i, 0:2, :] = mine[3, 2 * i : 2 * i + 2, :]
        gathered[i, 2:4, :] = theirs[3, 2 * i : 2 * i + 2, :]
        gathered[i, 4:6, :] = theirs[3, 2 * i : 2 * i + 2, :]
        gathered[i, 6:8, :] = mine[3, 2 * i : 2 * i + 2, :]
    grad = []
    vert = []
    for t in range(2):
        outer = gathered[t]
        other = row_roll(outer, 4)
        grad.append(outer - corner[t])
        vert.append(corner[2 + t] + gathered[2 + t] + corner[4] * (other - outer))
    flux = isoneutral(grad, vert, gathered[4])
    change[...] = jnp.zeros_like(change)
    for t in range(2):
        moved = flux[t] * gathered[5]
        for i in range(2):
            change[i, t, 0:1, :] = moved[2 * i : 2 * i + 1]
            change[i, t, X - 1 : X, :] = moved[2 * i + 1 : 2 * i + 2]
    own_tail = mine[2]
    own_ratio = 1.0 - own_tail
    scale = reciprocal(own_tail + own_ratio * theirs[2])
    last = tuple(
        (mine[t] + change[0, t] + own_ratio * (theirs[t] + change[1, t])) * scale for t in range(2)
    )
    edge = (K - 1) * (1 - slab)

    def copies(k):
        return [pltpu.make_async_copy(u.at[t, k], out.at[t, :, k, :], sems.at[t, k]) for t in range(2)]

    for t in range(2):
        u[t, edge] = last[t]
    for copy in copies(edge):
        copy.start()

    def backward(i, values):
        j = K - 2 - i
        k = jnp.where(slab == 0, j, K - 1 - j)
        rat = ratio[k]
        new = tuple(v[t, k] + rat * values[t] for t in range(2))
        for t in range(2):
            u[t, k] = new[t]
        for copy in copies(k):
            copy.start()
        return new

    lax.fori_loop(0, K - 1, backward, last)

    @pl.loop(0, K)
    def _(k):
        for copy in copies(k):
            copy.wait()


def shape(*dims):
    return jax.ShapeDtypeStruct(dims, F32)


def params(mib):
    return pltpu.CompilerParams(vmem_limit_bytes=mib * 1024 * 1024)


def local(
    tracers, zonal, merid, vertical, diffusivity, turbulence, sea, bottom
):
    count = lax.axis_size("tile")
    east_msg, west_msg, level_msg = pl.pallas_call(
        pack_kernel,
        name="pack",
        in_specs=[any_spec()] * 5 + [vmem_spec()] * 2,
        out_specs=[vmem_spec()] * 3,
        out_shape=[shape(4 * K + 8, Y), shape(6 * K + 8, Y), shape(5, X, Y)],
        scratch_shapes=[pltpu.VMEM((X, Y), F32), pltpu.SemaphoreType.DMA((24,))],
        compiler_params=params(60),
    )(tracers, zonal, vertical, diffusivity, turbulence, sea, bottom)

    eastward = [(i, (i + 1) % count) for i in range(count)]
    east_in = lax.ppermute(east_msg, "tile", eastward)
    west_in = lax.ppermute(west_msg, "tile", [(b, a) for a, b in eastward])
    level_in = lax.ppermute(level_msg, "lev", [(0, 1), (1, 0)])

    p, inverse, carry, ratio, tail, *pieces = pl.pallas_call(
        interior_kernel,
        name="interior",
        in_specs=[any_spec()] * 6 + [vmem_spec()] * 2,
        out_specs=[vmem_spec()] * 10,
        out_shape=[
            shape(2, LANES, K * X, 128), shape(K, X, Y), shape(K, X, Y), shape(K, X, Y), shape(2, X, Y),
            shape(2, 6, K, Y), shape(3, K, Y), shape(3, K, Y), shape(2, 3, X, Y), shape(4, X, Y),
        ],
        scratch_shapes=[
            pltpu.VMEM((2, K, X, Y), F32),
            pltpu.VMEM((K, X, Y), F32),
            pltpu.VMEM((K, X, Y), F32),
            pltpu.VMEM((K, X, Y), F32),
            pltpu.VMEM((K, X, Y), F32),
            pltpu.VMEM((K, X, Y), F32),
            pltpu.VMEM((2, X, Y), F32),
            pltpu.VMEM((K + 1, X, Y), F32),
            pltpu.SemaphoreType.DMA((6, K)),
            pltpu.SemaphoreType.DMA((18,)),
        ],
        compiler_params=params(50),
        cost_estimate=pl.CostEstimate(flops=50_000_000, bytes_accessed=40_000_000, transcendentals=0),
    )(tracers, zonal, merid, vertical, diffusivity, turbulence, sea, bottom)

    v, meet, corner = pl.pallas_call(
        edge_kernel,
        name="edges",
        in_specs=[vmem_spec()] * 5 + [any_spec()] + [vmem_spec()] * 8,
        out_specs=[vmem_spec()] * 3,
        out_shape=[shape(2, K, X, Y), shape(4, X, Y), shape(5, 8, Y)],
        scratch_shapes=[
            pltpu.VMEM((2, LANES, K * X, 128), F32),
            pltpu.VMEM((2, 5, X, Y), F32),
            pltpu.SemaphoreType.DMA,
        ],
        compiler_params=params(50),
    )(east_in, west_in, level_in, sea, bottom, p, inverse, carry, tail, *pieces)

    meet_in = lax.ppermute(meet, "lev", [(0, 1), (1, 0)])
    return pl.pallas_call(
        finish_kernel,
        name="finish",
        in_specs=[vmem_spec()] * 5,
        out_specs=any_spec(),
        out_shape=shape(2, X, K, Y),
        scratch_shapes=[
            pltpu.VMEM((2, K, X, Y), F32),
            pltpu.VMEM((6, 8, Y), F32),
            pltpu.VMEM((2, 2, X, Y), F32),
            pltpu.SemaphoreType.DMA((2, K)),
        ],
        compiler_params=params(50),
    )(v, ratio, meet, meet_in, corner)


def solution(mesh):
    return jax.shard_map(
        local,
        mesh=mesh,
        in_specs=(
            P(None, "tile", "lev", None),
            P("tile", "lev", None),
            P("tile", "lev", None),
            P("tile", "lev", None),
            P("tile", "lev", None),
            P("tile", "lev", None),
            P("tile", None),
            P("tile", None),
        ),
        out_specs=P(None, "tile", "lev", None),
        check_vma=False,
    )
```

time: 54.4 us -> 39.3 us (0.72)
  starting transfers between devices: 17 us -> 10.6 us
  local copies, waits for them, and re-layouts: 7.42 us -> 1.42 us
  Pallas kernels: 23.6 us -> 21.5 us
    ppermute x2 -> x0, starting transfers between devices: 7.18 us -> none  [the longest x1 7.17 us: local(): west_corner_in = lax.ppermute(west_corner, ('tile', 'lev'), west_cross)]
    unnamed x16 -> x6, local copies, waits for them, and re-layouts: 7.42 us -> 1.42 us
    pallas_call x1, Pallas kernels: 16.8 us -> 12.7 us  [local(): pl.pallas_call(interior_kernel, name='interior', in_specs=[any_spec()] *...]
    pallas_call x1, Pallas kernels: 1.02 us -> 2.92 us  [local(): pl.pallas_call(pack_kernel, name='pack', in_specs=[any_spec()] * 5 + [vme...]
    ppermute x1, starting transfers between devices: 0.09 us -> 0.87 us  [local(): meet_in = lax.ppermute(meet, 'lev', [(0, 1), (1, 0)])]
  transfers between devices with their start and end apart: 6 -> 4, of which waited for: 1 -> 1; matrix products, arithmetic and copies ran while one was open for 0% -> 0% of each run, Pallas kernels for 31% -> 33%
where the time goes in v1:
time: 39.3 us; the launch traced here: 38.9 us
  Pallas kernels  21.5 us (55%)
  starting transfers between devices  10.6 us (27%)
  waiting for transfers between devices  5.34 us (14%)
  local copies, waits for them, and re-layouts  1.42 us (4%)
    pallas_call x1, Pallas kernels, local(): pl.pallas_call(interior_kernel, name='interior', in_specs=[any_spec()] *...  12.7 us
    ppermute x1, starting transfers between devices, local(): west_in = lax.ppermute(west_msg, 'tile', [(b, a) for a, b in eastward])  7.01 us
    ppermute x1, waiting for transfers between devices, local(): meet_in = lax.ppermute(meet, 'lev', [(0, 1), (1, 0)])  5.33 us
    pallas_call x1, Pallas kernels, local(): pl.pallas_call(edge_kernel, name='edges', in_specs=[vmem_spec()] * 5 + [a...  3.82 us
    pallas_call x1, Pallas kernels, local(): pl.pallas_call(pack_kernel, name='pack', in_specs=[any_spec()] * 5 + [vme...  2.92 us
    ppermute x1, starting transfers between devices, local(): level_in = lax.ppermute(level_msg, 'lev', [(0, 1), (1, 0)])  2.73 us
    pallas_call x1, Pallas kernels, local(): pl.pallas_call(finish_kernel, name='finish', in_specs=[vmem_spec()] * 5,...  2.04 us
    unnamed x6, local copies, waits for them, and re-layouts  1.42 us
  transfers between devices with their start and end apart: 4, of which 1 were waited for; matrix products, arithmetic and copies ran while one was open for 0% of the time, Pallas kernels for 33%

profile of v1, /device:TPU:0, one launch (start us, length us, event | category | flops | bytes accessed | tf_op | source)
XLA Modules:
  0.0 38.9 jit_solution(5746816290341584764)
XLA Ops:
  0.0 0.0 copy-start.2
  0.0 0.0 copy-start.1
  0.0 2.9 %pack.1 = (f32[136,384]{1,0:T(8,128)}, f32[200,384]{1,0:T(8,128)}, f32[5,16,384]{2,1,0:T(8,128)}) custom-call(f32[2,16,32,384]{3,2,1,0:T(8,128)} %tracers.3, f32[16,32,384]{2,1,0:T(8,128)} %zonal.3, f32[16,32,384]{2,1,0:T(8,128)} %vertical.3, f32[16,32,384]{2,1,0:T(8,128)} %diffusivity.3, f32[16,32,384]{2,1,0:T(8,128)} %turbulence.3, s32[16,384]{1,0:T(8,128)} %sea.5, ...), custom_call_target="tpu_custom_call" | custom-call | tf_op jit(solution)/shard_map/pack/pallas_call | solution.py:565
  2.9 7.0 %collective-permute-start.1 = (f32[200,384]{1,0:T(8,128)}, f32[200,384]{1,0:T(8,128)S(1)}, u32[]{:S(2)}, u32[]{:S(2)}) collective-permute-start(f32[200,384]{1,0:T(8,128)} %get-tuple-element.22), channel_id=1, source_target_pairs={{2,0},{4,2},{6,4},{8,6},{10,8},{12,10},{14,12},{16,14},{18,16},{20... | collective-permute-start | bytes 921608 | tf_op jit(solution)/shard_map/ppermute | solution.py:577
  10.0 0.0 collective-permute-start
  10.0 2.7 %collective-permute-start.2 = (f32[5,16,384]{2,1,0:T(8,128)}, f32[5,16,384]{2,1,0:T(8,128)S(1)}, u32[]{:S(2)}, u32[]{:S(2)}) collective-permute-start(f32[5,16,384]{2,1,0:T(8,128)} %get-tuple-element.23), channel_id=1, source_target_pairs={{0,1},{1,0},{2,3},{3,2},{4,5},{5,4},{6,7},{7,6},{8,9},{9,8},{10,11... | collective-permute-start | bytes 368648 | tf_op jit(solution)/shard_map/ppermute | solution.py:578
  12.7 0.0 copy-done.2
  12.7 0.0 copy-done.1
  12.7 12.7 %interior.1 = (f32[2,3,512,128]{3,2,1,0:T(8,128)}, f32[32,16,384]{2,1,0:T(8,128)S(1)}, f32[32,16,384]{2,1,0:T(8,128)S(1)}, f32[32,16,384]{2,1,0:T(8,128)S(1)}, f...) custom-call(f32[2,16,32,384]{3,2,1,0:T(8,128)} %tracers.3, ...), custom_call_target="tpu_custom_call" | custom-call | flops 50000000 | bytes 40000000 | tf_op jit(solution)/shard_map/interior/pallas_call | solution.py:580
  25.4 0.0 collective-permute-done.2.level_msg
  25.4 0.0 collective-permute-done.east_msg
  25.4 0.0 collective-permute-done.1.west_msg
  25.4 3.8 %edges.1 = (f32[2,32,16,384]{3,2,1,0:T(8,128)}, f32[4,16,384]{2,1,0:T(8,128)S(1)}, f32[5,8,384]{2,1,0:T(8,128)S(1)}) custom-call(f32[136,384]{1,0:T(8,128)S(1)} %collective-permute-done.east_msg, f32[200,384]{1,0:T(8,128)S(1)} %collective-permute-done.1.west_msg, f32[5,16,384]{2,1,0:T(8,128)S(1)} %collective-permute-done.2.level_msg, ...), custom_call_target="tpu_custom_call" | custom-call | tf_op jit(solution)/shard_map/edges/pallas_call | solution.py:605
  29.3 0.9 %collective-permute-start.3 = (f32[4,16,384]{2,1,0:T(8,128)S(1)}, f32[4,16,384]{2,1,0:T(8,128)S(1)}, u32[]{:S(2)}, u32[]{:S(2)}) collective-permute-start(f32[4,16,384]{2,1,0:T(8,128)S(1)} %get-tuple-element.35.mine), channel_id=1, source_target_pairs={{0,1},{1,0},{2,3},{3,2},{4,5},{5,4},{6,7},{7,6},{8,9},{9,8},{10,11... | collective-permute-start | bytes 294920 | tf_op jit(solution)/shard_map/ppermute | solution.py:619
  30.1 5.3 %collective-permute-done.3.theirs = f32[4,16,384]{2,1,0:T(8,128)S(1)} collective-permute-done((f32[4,16,384]{2,1,0:T(8,128)S(1)}, f32[4,16,384]{2,1,0:T(8,128)S(1)}, u32[]{:S(2)}, u32[]{:S(2)}) %collective-permute-start.3) | collective-permute-done | bytes 98336 | tf_op jit(solution)/shard_map/ppermute | solution.py:619
  35.5 0.0 copy-start
  35.5 1.4 %copy-done = f32[2,32,16,384]{3,2,1,0:T(8,128)S(1)} copy-done((f32[2,32,16,384]{3,2,1,0:T(8,128)S(1)}, f32[2,32,16,384]{3,2,1,0:T(8,128)}, u32[]{:S(2)}) %copy-start) | copy-done | bytes 1572888
  36.9 2.0 %finish.1 = f32[2,16,32,384]{3,2,1,0:T(8,128)} custom-call(f32[2,32,16,384]{3,2,1,0:T(8,128)S(1)} %copy-done, f32[32,16,384]{2,1,0:T(8,128)S(1)} %get-tuple-element.34.ratio, f32[4,16,384]{2,1,0:T(8,128)S(1)} %get-tuple-element.35.mine, f32[4,16,384]{2,1,0:T(8,128)S(1)} %collective-permute-done.3.theirs, f32[5,8,384]{2,1,0:T(8,128)S(1)} %get-tuple-element.36.corner), custom_call_target="tpu_custom_call" | custom-call | tf_op jit(solution)/shard_map/finish/pallas_call | solution.py:620
Async XLA Ops:
  0.0 12.7 %copy-start.2 = (s32[16,384]{1,0:T(8,128)S(1)}, s32[16,384]{1,0:T(8,128)}, u32[]{:S(2)}) copy-start(s32[16,384]{1,0:T(8,128)} %bottom.5) | copy-start | bytes 73732
  0.0 12.7 %copy-start.1 = (s32[16,384]{1,0:T(8,128)S(1)}, s32[16,384]{1,0:T(8,128)}, u32[]{:S(2)}) copy-start(s32[16,384]{1,0:T(8,128)} %sea.5) | copy-start | bytes 73732
  2.9 22.5 %collective-permute-start.1 = (f32[200,384]{1,0:T(8,128)}, f32[200,384]{1,0:T(8,128)S(1)}, u32[]{:S(2)}, u32[]{:S(2)}) collective-permute-start(f32[200,384]{1,0:T(8,128)} %get-tuple-element.22), channel_id=1, source_target_pairs={{2,0},{4,2},{6,4},{8,6},{10,8},{12,10},{14,12},{16,14},{18,16},{20... | collective-permute-start | bytes 921608 | tf_op jit(solution)/shard_map/ppermute | solution.py:577
  10.0 15.5 %collective-permute-start = (f32[136,384]{1,0:T(8,128)}, f32[136,384]{1,0:T(8,128)S(1)}, u32[]{:S(2)}, u32[]{:S(2)}) collective-permute-start(f32[136,384]{1,0:T(8,128)} %get-tuple-element.21), channel_id=1, source_target_pairs={{0,2},{2,4},{4,6},{6,8},{8,10},{10,12},{12,14},{14,16},{16,18},{18... | collective-permute-start | bytes 626696 | tf_op jit(solution)/shard_map/ppermute | solution.py:576
  10.0 15.4 %collective-permute-start.2 = (f32[5,16,384]{2,1,0:T(8,128)}, f32[5,16,384]{2,1,0:T(8,128)S(1)}, u32[]{:S(2)}, u32[]{:S(2)}) collective-permute-start(f32[5,16,384]{2,1,0:T(8,128)} %get-tuple-element.23), channel_id=1, source_target_pairs={{0,1},{1,0},{2,3},{3,2},{4,5},{5,4},{6,7},{7,6},{8,9},{9,8},{10,11... | collective-permute-start | bytes 368648 | tf_op jit(solution)/shard_map/ppermute | solution.py:578
  29.3 6.2 %collective-permute-start.3 = (f32[4,16,384]{2,1,0:T(8,128)S(1)}, f32[4,16,384]{2,1,0:T(8,128)S(1)}, u32[]{:S(2)}, u32[]{:S(2)}) collective-permute-start(f32[4,16,384]{2,1,0:T(8,128)S(1)} %get-tuple-element.35.mine), channel_id=1, source_target_pairs={{0,1},{1,0},{2,3},{3,2},{4,5},{5,4},{6,7},{7,6},{8,9},{9,8},{10,11... | collective-permute-start | bytes 294920 | tf_op jit(solution)/shard_map/ppermute | solution.py:619
  35.5 1.4 %copy-start = (f32[2,32,16,384]{3,2,1,0:T(8,128)S(1)}, f32[2,32,16,384]{3,2,1,0:T(8,128)}, u32[]{:S(2)}) copy-start(f32[2,32,16,384]{3,2,1,0:T(8,128)} %get-tuple-element.33.v) | copy-start | bytes 4718596

commit v2 on v1

--- a/solution.py
+++ b/solution.py
@@ -121,8 +121,8 @@
 
 def interior_kernel(
     tracers, zonal, merid, vertical, diffusivity, turbulence, sea, bottom,
-    p_out, inverse_out, carry_out, ratio_out, tail_out, cols, zcols, dcols, own_rows, extra_rows,
-    q, zc, mc, vc, df, tb, below_flux, rate, sems, col_sems
+    p_first, p_second, inverse_out, carry_out, ratio_out, tail_out, cols, zcols, dcols, own_rows, extra_rows,
+    q, zc, mc, vc, df, tb, below_flux, grads_kept, sems, col_sems
 ):
     slab = lax.axis_index("lev")
     edge = (K - 1) * (1 - slab)
@@ -135,7 +135,7 @@
             (merid.at[:, k, :], mc.at[k]),
             (vertical.at[:, k, :], vc.at[k]),
             (diffusivity.at[:, k, :], df.at[k]),
-            (turbulence.at[:, k, :], tb.at[k]),
+            (turbulence.at[:, jnp.where(slab == 0, k, jnp.maximum(K - 2 - k, 0)), :], tb.at[k]),
         ]
         return [pltpu.make_async_copy(a, b, sems.at[i, k]) for i, (a, b) in enumerate(pairs)]
 
@@ -161,24 +161,33 @@
         add(zonal.at[x], zcols.at[i])
         add(diffusivity.at[x], dcols.at[i])
     below_flux[...] = jnp.zeros_like(below_flux)
-    rate[0] = jnp.zeros((X, Y), F32)
+    tail_out[...] = jnp.zeros_like(tail_out)
+    grads_kept[0] = jnp.zeros((2, X, Y), F32)
 
     for k in range(2):
         for copy in copies(k):
             copy.wait()
-
-    def process(k, below):
+    for t in range(2):
+        grads_kept[1, t] = jnp.where(base + 1 < depth, q[t, 1] - q[t, 0], 0.0)
+
+    def eliminate(j, tail, prev_rate):
+        face = jnp.where(slab == 0, j + 1, 2 * K - 1 - j)
+        turb = tb[j]
+        next_rate = jnp.where(face < depth, turb * lax.rsqrt(turb), 0.0)
+        rest = 1.0 + prev_rate * tail
+        inverse = reciprocal(rest + next_rate)
+        inverse_out[j] = inverse
+        carry_out[j] = prev_rate * inverse
+        ratio_out[j] = next_rate * inverse
+        return rest * inverse, next_rate
+
+    def process(k, below, grad_up, grad_down):
         ahead = jnp.minimum(k + 2, K - 1)
         level = base + k
-        up = jnp.maximum(k - 1, 0)
         down = jnp.minimum(k + 1, K - 1)
         here = [q[t, k] for t in range(2)]
         next_row = [q[t, down] for t in range(2)]
-        open_up = jnp.where(k > 0, level, FAR) < depth
-        open_down = jnp.where(k < K - 1, level + 1, FAR) < depth
         open_far = jnp.where(k < K - 2, level + 2, FAR) < depth
-        grad_up = [jnp.where(open_up, here[t] - q[t, up], 0.0) for t in range(2)]
-        grad_down = [jnp.where(open_down, next_row[t] - here[t], 0.0) for t in range(2)]
         grad_far = [jnp.where(open_far, q[t, ahead] - next_row[t], 0.0) for t in range(2)]
         centred = [grad_up[t] + grad_down[t] for t in range(2)]
         known = jnp.where(slab == 0, k < K - 2, k > 0)
@@ -188,7 +197,6 @@
         total = []
         for t in range(2):
             total.append(here[t] + below[t] - vert[t])
-        rate[k + 1] = jnp.where(level + 1 < depth, tb[k] * lax.rsqrt(tb[k]), 0.0)
         iso_level = jnp.where(k == edge, FAR, level)
         spread = df[k]
 
@@ -230,44 +238,45 @@
             net = iso[t] - flux[t]
             total[t] = total[t] + (lane_roll(net, -1) - net)
             for lane in range(LANES):
-                p_out[t, lane, pl.ds(k * X, X), :] = total[t][:, lane * 128 : lane * 128 + 128]
-        return vert
-
-    @pl.loop(0, K // UNROLL)
-    def _(i):
+                (p_first, p_second)[t][lane, pl.ds(k * X, X), :] = total[t][:, lane * 128 : lane * 128 + 128]
+        return vert, grad_down, grad_far
+
+    def step(i, start, wait):
         first = i * UNROLL
         for u in range(UNROLL):
-            @pl.when(first + u + AHEAD < K)
-            def _():
+            if start:
                 for copy in copies(first + u + AHEAD):
                     copy.start()
-
-            @pl.when(first + u + 2 < K)
-            def _():
+            if wait:
                 for copy in copies(first + u + 2):
                     copy.wait()
-
         below = [below_flux[t] for t in range(2)]
+        grads = [[grads_kept[f, t] for t in range(2)] for f in range(2)]
+        tail, prev_rate = tail_out[0], tail_out[1]
         for u in range(UNROLL):
-            below = process(first + u, below)
+            below, grad_down, grad_far = process(first + u, below, grads[0], grads[1])
+            grads = [grad_down, grad_far]
+            if wait or u < UNROLL - 1:
+                tail, prev_rate = eliminate(first + u, tail, prev_rate)
         for t in range(2):
             below_flux[t] = below[t]
-
-    def eliminate(j, tail):
-        prev_face = jnp.where(slab == 0, j, K - j)
-        next_face = jnp.where(slab == 0, j + 1, K - 1 - j)
-        k = jnp.where(slab == 0, j, K - 1 - j)
-        prev_rate = rate[prev_face]
-        next_rate = rate[next_face]
-        rest = 1.0 + prev_rate * tail
-        inverse = reciprocal(rest + next_rate)
-        inverse_out[k] = inverse
-        carry_out[k] = prev_rate * inverse
-        ratio_out[k] = next_rate * inverse
-        return rest * inverse
-
-    tail_out[0] = lax.fori_loop(0, K - 1, eliminate, jnp.zeros((X, Y), F32))
-    tail_out[1] = rate[jnp.where(slab == 0, K - 1, 1)]
+            for f in range(2):
+                grads_kept[f, t] = grads[f][t]
+        tail_out[0] = tail
+        tail_out[1] = prev_rate
+
+    steps = K // UNROLL
+    fed = (K - AHEAD) // UNROLL
+
+    @pl.loop(0, fed)
+    def _(i):
+        step(i, True, True)
+
+    @pl.loop(fed, steps - 1)
+    def _(i):
+        step(i, False, True)
+
+    step(steps - 1, False, False)
     for t in range(2):
         for i in range(3):
             own_rows[t, i] = q[t, (K - 3) * (1 - slab) + i]
@@ -281,16 +290,19 @@
 
 def edge_kernel(
     east_msg, west_msg, level_msg, sea, bottom,
-    p_in, inverse, carry, tail, cols, zcols, dcols, own_rows, extra_rows,
-    v_out, meet_out, corner_out,
-    p, rows, sem
+    p_first, p_second, inverse, carry, tail, cols, zcols, dcols, own_rows, extra_rows,
+    v_first, v_second, meet_out, corner_out,
+    p, rows, sems
 ):
     slab = lax.axis_index("lev")
     edge = (K - 1) * (1 - slab)
     inner = 30 - 29 * slab
     base = K * slab
-    fetch = pltpu.make_async_copy(p_in, p, sem)
-    fetch.start()
+    fetches = [
+        pltpu.make_async_copy(ref, p.at[t], sems.at[t]) for t, ref in enumerate((p_first, p_second))
+    ]
+    for fetch in fetches:
+        fetch.start()
     for t in range(2):
         for i in range(3):
             rows[t, 2 * slab + i] = own_rows[t, i]
@@ -363,7 +375,8 @@
         [dcols[0], dcols[1]],
         0,
     )
-    fetch.wait()
+    for fetch in fetches:
+        fetch.wait()
     for t in range(2):
         add_column(t, 0, nets[1][t] - nets[0][t])
         add_column(t, 1, -nets[1][t])
@@ -438,11 +451,11 @@
 
     def forward(j, values):
         k = jnp.where(slab == 0, j, K - 1 - j)
-        inv = inverse[k]
-        car = carry[k]
+        inv = inverse[j]
+        car = carry[j]
         new = tuple(provisional(t, k) * inv + car * values[t] for t in range(2))
         for t in range(2):
-            v_out[t, k] = new[t]
+            (v_first, v_second)[t][k] = new[t]
         return new
 
     zero = jnp.zeros((X, Y), F32)
@@ -494,7 +507,7 @@
         corner_out[4, 2 + side : 3 + side, :] = shared
 
 
-def finish_kernel(v, ratio, mine, theirs, corner, out, u, gathered, change, sems):
+def finish_kernel(v_first, v_second, ratio, mine, theirs, corner, out, u, gathered, change, sems):
     slab = lax.axis_index("lev")
     for i in range(6):
         gathered[i, 0:2, :] = mine[3, 2 * i : 2 * i + 2, :]
@@ -534,8 +547,8 @@
     def backward(i, values):
         j = K - 2 - i
         k = jnp.where(slab == 0, j, K - 1 - j)
-        rat = ratio[k]
-        new = tuple(v[t, k] + rat * values[t] for t in range(2))
+        rat = ratio[j]
+        new = tuple(v[k] + rat * values[t] for t, v in enumerate((v_first, v_second)))
         for t in range(2):
             u[t, k] = new[t]
         for copy in copies(k):
@@ -577,13 +590,14 @@
     west_in = lax.ppermute(west_msg, "tile", [(b, a) for a, b in eastward])
     level_in = lax.ppermute(level_msg, "lev", [(0, 1), (1, 0)])
 
-    p, inverse, carry, ratio, tail, *pieces = pl.pallas_call(
+    p_first, p_second, inverse, carry, ratio, tail, *pieces = pl.pallas_call(
         interior_kernel,
         name="interior",
         in_specs=[any_spec()] * 6 + [vmem_spec()] * 2,
-        out_specs=[vmem_spec()] * 10,
+        out_specs=[vmem_spec()] * 11,
         out_shape=[
-            shape(2, LANES, K * X, 128), shape(K, X, Y), shape(K, X, Y), shape(K, X, Y), shape(2, X, Y),
+            shape(LANES, K * X, 128), shape(LANES, K * X, 128), shape(K, X, Y), shape(K, X, Y), shape(K, X, Y),
+            shape(2, X, Y),
             shape(2, 6, K, Y), shape(3, K, Y), shape(3, K, Y), shape(2, 3, X, Y), shape(4, X, Y),
         ],
         scratch_shapes=[
@@ -594,33 +608,33 @@
             pltpu.VMEM((K, X, Y), F32),
             pltpu.VMEM((K, X, Y), F32),
             pltpu.VMEM((2, X, Y), F32),
-            pltpu.VMEM((K + 1, X, Y), F32),
+            pltpu.VMEM((2, 2, X, Y), F32),
             pltpu.SemaphoreType.DMA((6, K)),
             pltpu.SemaphoreType.DMA((18,)),
         ],
-        compiler_params=params(50),
+        compiler_params=params(48),
         cost_estimate=pl.CostEstimate(flops=50_000_000, bytes_accessed=40_000_000, transcendentals=0),
     )(tracers, zonal, merid, vertical, diffusivity, turbulence, sea, bottom)
 
-    v, meet, corner = pl.pallas_call(
+    v_first, v_second, meet, corner = pl.pallas_call(
         edge_kernel,
         name="edges",
-        in_specs=[vmem_spec()] * 5 + [any_spec()] + [vmem_spec()] * 8,
-        out_specs=[vmem_spec()] * 3,
-        out_shape=[shape(2, K, X, Y), shape(4, X, Y), shape(5, 8, Y)],
+        in_specs=[vmem_spec()] * 15,
+        out_specs=[vmem_spec()] * 4,
+        out_shape=[shape(K, X, Y), shape(K, X, Y), shape(4, X, Y), shape(5, 8, Y)],
         scratch_shapes=[
             pltpu.VMEM((2, LANES, K * X, 128), F32),
             pltpu.VMEM((2, 5, X, Y), F32),
-            pltpu.SemaphoreType.DMA,
+            pltpu.SemaphoreType.DMA((2,)),
         ],
-        compiler_params=params(50),
-    )(east_in, west_in, level_in, sea, bottom, p, inverse, carry, tail, *pieces)
+        compiler_params=params(46),
+    )(east_in, west_in, level_in, sea, bottom, p_first, p_second, inverse, carry, tail, *pieces)
 
     meet_in = lax.ppermute(meet, "lev", [(0, 1), (1, 0)])
     return pl.pallas_call(
         finish_kernel,
         name="finish",
-        in_specs=[vmem_spec()] * 5,
+        in_specs=[vmem_spec()] * 6,
         out_specs=any_spec(),
         out_shape=shape(2, X, K, Y),
         scratch_shapes=[
@@ -629,8 +643,8 @@
             pltpu.VMEM((2, 2, X, Y), F32),
             pltpu.SemaphoreType.DMA((2, K)),
         ],
-        compiler_params=params(50),
-    )(v, ratio, meet, meet_in, corner)
+        compiler_params=params(46),
+    )(v_first, v_second, ratio, meet, meet_in, corner)
 
 
 def solution(mesh):

time: 39.3 us -> 34 us (0.87)
  Pallas kernels: 21.5 us -> 17.7 us
  local copies, waits for them, and re-layouts: 1.42 us -> 0.01 us
    pallas_call x2, Pallas kernels: 5.86 us -> 3.84 us  [the longest x1 2.06 us: local(): pl.pallas_call(finish_kernel, name='finish', in_specs=[vmem_spec()] * 6,...]
    pallas_call x1, Pallas kernels: 12.7 us -> 11 us  [local(): pl.pallas_call(interior_kernel, name='interior', in_specs=[any_spec()] *...]
    unnamed x6, local copies, waits for them, and re-layouts: 1.42 us -> 0.01 us
  transfers between devices with their start and end apart: 4 -> 4, of which waited for: 1 -> 1; matrix products, arithmetic and copies ran while one was open for 0% -> 0% of each run, Pallas kernels for 33% -> 32%
where the time goes in v2:
time: 34 us; the launch traced here: 33.8 us
  Pallas kernels  17.7 us (52%)
  starting transfers between devices  10.6 us (31%)
  waiting for transfers between devices  5.34 us (16%)
    pallas_call x1, Pallas kernels, local(): pl.pallas_call(interior_kernel, name='interior', in_specs=[any_spec()] *...  11 us
    ppermute x1, starting transfers between devices, local(): west_in = lax.ppermute(west_msg, 'tile', [(b, a) for a, b in eastward])  7.03 us
    ppermute x1, waiting for transfers between devices, local(): meet_in = lax.ppermute(meet, 'lev', [(0, 1), (1, 0)])  5.33 us
    pallas_call x1, Pallas kernels, local(): pl.pallas_call(pack_kernel, name='pack', in_specs=[any_spec()] * 5 + [vme...  2.92 us
    ppermute x1, starting transfers between devices, local(): level_in = lax.ppermute(level_msg, 'lev', [(0, 1), (1, 0)])  2.73 us
    pallas_call x1, Pallas kernels, local(): pl.pallas_call(finish_kernel, name='finish', in_specs=[vmem_spec()] * 6,...  2.06 us
    pallas_call x1, Pallas kernels, local(): pl.pallas_call(edge_kernel, name='edges', in_specs=[vmem_spec()] * 15, ou...  1.79 us
    ppermute x1, starting transfers between devices, local(): meet_in = lax.ppermute(meet, 'lev', [(0, 1), (1, 0)])  0.87 us
  transfers between devices with their start and end apart: 4, of which 1 were waited for; matrix products, arithmetic and copies ran while one was open for 0% of the time, Pallas kernels for 32%

profile of v2, /device:TPU:0, one launch (start us, length us, event | category | flops | bytes accessed | tf_op | source)
XLA Modules:
  0.0 33.8 jit_solution(17467030621434538848)
XLA Ops:
  0.0 0.0 copy-start.2
  0.0 0.0 copy-start.1
  0.0 0.0 copy-start
  0.0 2.9 %pack.1 = (f32[136,384]{1,0:T(8,128)}, f32[200,384]{1,0:T(8,128)}, f32[5,16,384]{2,1,0:T(8,128)}) custom-call(f32[2,16,32,384]{3,2,1,0:T(8,128)} %tracers.3, f32[16,32,384]{2,1,0:T(8,128)} %zonal.3, f32[16,32,384]{2,1,0:T(8,128)} %vertical.3, f32[16,32,384]{2,1,0:T(8,128)} %diffusivity.3, f32[16,32,384]{2,1,0:T(8,128)} %turbulence.3, s32[16,384]{1,0:T(8,128)} %sea.5, ...), custom_call_target="tpu_custom_call" | custom-call | tf_op jit(solution)/shard_map/pack/pallas_call | solution.py:578
  2.9 7.0 %collective-permute-start.1 = (f32[200,384]{1,0:T(8,128)}, f32[200,384]{1,0:T(8,128)S(1)}, u32[]{:S(2)}, u32[]{:S(2)}) collective-permute-start(f32[200,384]{1,0:T(8,128)} %get-tuple-element.24), channel_id=1, source_target_pairs={{2,0},{4,2},{6,4},{8,6},{10,8},{12,10},{14,12},{16,14},{18,16},{20... | collective-permute-start | bytes 921608 | tf_op jit(solution)/shard_map/ppermute | solution.py:590
  10.0 0.0 collective-permute-start
  10.0 2.7 %collective-permute-start.2 = (f32[5,16,384]{2,1,0:T(8,128)}, f32[5,16,384]{2,1,0:T(8,128)S(1)}, u32[]{:S(2)}, u32[]{:S(2)}) collective-permute-start(f32[5,16,384]{2,1,0:T(8,128)} %get-tuple-element.25), channel_id=1, source_target_pairs={{0,1},{1,0},{2,3},{3,2},{4,5},{5,4},{6,7},{7,6},{8,9},{9,8},{10,11... | collective-permute-start | bytes 368648 | tf_op jit(solution)/shard_map/ppermute | solution.py:591
  12.7 0.0 copy-done.2
  12.7 0.0 copy-done.1
  12.7 0.0 copy-done
  12.7 11.0 %interior.1 = (f32[3,512,128]{2,1,0:T(8,128)S(1)}, f32[3,512,128]{2,1,0:T(8,128)S(1)}, f32[32,16,384]{2,1,0:T(8,128)S(1)}, f32[32,16,384]{2,1,0:T(8,128)S(1)}, f...) custom-call(f32[2,16,32,384]{3,2,1,0:T(8,128)} %tracers.3, ...), custom_call_target="tpu_custom_call" | custom-call | flops 50000000 | bytes 40000000 | tf_op jit(solution)/shard_map/interior/pallas_call | solution.py:593
  23.7 0.0 collective-permute-done.2.level_msg
  23.7 0.0 collective-permute-done.east_msg
  23.7 0.0 collective-permute-done.1.west_msg
  23.7 1.8 %edges.1 = (f32[32,16,384]{2,1,0:T(8,128)S(1)}, f32[32,16,384]{2,1,0:T(8,128)S(1)}, f32[4,16,384]{2,1,0:T(8,128)S(1)}, f32[5,8,384]{2,1,0:T(8,128)S(1)}) custom-call(f32[136,384]{1,0:T(8,128)S(1)} %collective-permute-done.east_msg, f32[200,384]{1,0:T(8,128)S(1)} %collective-permute-done.1.west_msg, f32[5,16,384]{2,1,0:T(8,128)S(1)} %collective-permute-done.2.level_msg, ...), custom_call_target="tpu_custom_call" | custom-call | tf_op jit(solution)/shard_map/edges/pallas_call | solution.py:619
  25.5 0.9 %collective-permute-start.3 = (f32[4,16,384]{2,1,0:T(8,128)S(1)}, f32[4,16,384]{2,1,0:T(8,128)S(1)}, u32[]{:S(2)}, u32[]{:S(2)}) collective-permute-start(f32[4,16,384]{2,1,0:T(8,128)S(1)} %get-tuple-element.39.mine), channel_id=1, source_target_pairs={{0,1},{1,0},{2,3},{3,2},{4,5},{5,4},{6,7},{7,6},{8,9},{9,8},{10,11... | collective-permute-start | bytes 294920 | tf_op jit(solution)/shard_map/ppermute | solution.py:633
  26.4 5.3 %collective-permute-done.3.theirs = f32[4,16,384]{2,1,0:T(8,128)S(1)} collective-permute-done((f32[4,16,384]{2,1,0:T(8,128)S(1)}, f32[4,16,384]{2,1,0:T(8,128)S(1)}, u32[]{:S(2)}, u32[]{:S(2)}) %collective-permute-start.3) | collective-permute-done | bytes 98336 | tf_op jit(solution)/shard_map/ppermute | solution.py:633
  31.7 2.1 %finish.1 = f32[2,16,32,384]{3,2,1,0:T(8,128)} custom-call(f32[32,16,384]{2,1,0:T(8,128)S(1)} %get-tuple-element.36.v_first, f32[32,16,384]{2,1,0:T(8,128)S(1)} %get-tuple-element.37.v_second, f32[32,16,384]{2,1,0:T(8,128)S(1)} %get-tuple-element.38.ratio, f32[4,16,384]{2,1,0:T(8,128)S(1)} %get-tuple-element.39.mine, ...), custom_call_target="tpu_custom_call" | custom-call | tf_op jit(solution)/shard_map/finish/pallas_call | solution.py:634
Async XLA Ops:
  0.0 12.7 %copy-start.2 = (s32[16,384]{1,0:T(8,128)S(1)}, s32[16,384]{1,0:T(8,128)}, u32[]{:S(2)}) copy-start(s32[16,384]{1,0:T(8,128)} %bottom.5) | copy-start | bytes 73732
  0.0 12.7 %copy-start.1 = (s32[16,384]{1,0:T(8,128)S(1)}, s32[16,384]{1,0:T(8,128)}, u32[]{:S(2)}) copy-start(s32[16,384]{1,0:T(8,128)} %sea.5) | copy-start | bytes 73732
  0.0 12.7 %copy-start = (f32[16,32,384]{2,1,0:T(8,128)S(1)}, f32[16,32,384]{2,1,0:T(8,128)}, u32[]{:S(2)}) copy-start(f32[16,32,384]{2,1,0:T(8,128)} %zonal.3) | copy-start | bytes 2359300
  2.9 20.8 %collective-permute-start.1 = (f32[200,384]{1,0:T(8,128)}, f32[200,384]{1,0:T(8,128)S(1)}, u32[]{:S(2)}, u32[]{:S(2)}) collective-permute-start(f32[200,384]{1,0:T(8,128)} %get-tuple-element.24), channel_id=1, source_target_pairs={{2,0},{4,2},{6,4},{8,6},{10,8},{12,10},{14,12},{16,14},{18,16},{20... | collective-permute-start | bytes 921608 | tf_op jit(solution)/shard_map/ppermute | solution.py:590
  10.0 13.7 %collective-permute-start = (f32[136,384]{1,0:T(8,128)}, f32[136,384]{1,0:T(8,128)S(1)}, u32[]{:S(2)}, u32[]{:S(2)}) collective-permute-start(f32[136,384]{1,0:T(8,128)} %get-tuple-element.23), channel_id=1, source_target_pairs={{0,2},{2,4},{4,6},{6,8},{8,10},{10,12},{12,14},{14,16},{16,18},{18... | collective-permute-start | bytes 626696 | tf_op jit(solution)/shard_map/ppermute | solution.py:589
  10.0 13.7 %collective-permute-start.2 = (f32[5,16,384]{2,1,0:T(8,128)}, f32[5,16,384]{2,1,0:T(8,128)S(1)}, u32[]{:S(2)}, u32[]{:S(2)}) collective-permute-start(f32[5,16,384]{2,1,0:T(8,128)} %get-tuple-element.25), channel_id=1, source_target_pairs={{0,1},{1,0},{2,3},{3,2},{4,5},{5,4},{6,7},{7,6},{8,9},{9,8},{10,11... | collective-permute-start | bytes 368648 | tf_op jit(solution)/shard_map/ppermute | solution.py:591
  25.5 6.2 %collective-permute-start.3 = (f32[4,16,384]{2,1,0:T(8,128)S(1)}, f32[4,16,384]{2,1,0:T(8,128)S(1)}, u32[]{:S(2)}, u32[]{:S(2)}) collective-permute-start(f32[4,16,384]{2,1,0:T(8,128)S(1)} %get-tuple-element.39.mine), channel_id=1, source_target_pairs={{0,1},{1,0},{2,3},{3,2},{4,5},{5,4},{6,7},{7,6},{8,9},{9,8},{10,11... | collective-permute-start | bytes 294920 | tf_op jit(solution)/shard_map/ppermute | solution.py:633

commit v3 on v2

--- a/solution.py
+++ b/solution.py
@@ -122,22 +122,26 @@
 def interior_kernel(
     tracers, zonal, merid, vertical, diffusivity, turbulence, sea, bottom,
     p_first, p_second, inverse_out, carry_out, ratio_out, tail_out, cols, zcols, dcols, own_rows, extra_rows,
-    q, zc, mc, vc, df, tb, below_flux, grads_kept, sems, col_sems
+    fields, below_flux, grads_kept, sems, col_sems
 ):
     slab = lax.axis_index("lev")
     edge = (K - 1) * (1 - slab)
     base = K * slab
 
     def copies(k):
+        turned = jnp.where(slab == 0, k, jnp.maximum(K - 2 - k, 0))
         pairs = [
-            (tracers.at[:, :, k, :], q.at[:, k]),
-            (zonal.at[:, k, :], zc.at[k]),
-            (merid.at[:, k, :], mc.at[k]),
-            (vertical.at[:, k, :], vc.at[k]),
-            (diffusivity.at[:, k, :], df.at[k]),
-            (turbulence.at[:, jnp.where(slab == 0, k, jnp.maximum(K - 2 - k, 0)), :], tb.at[k]),
+            (tracers.at[:, :, k, :], fields.at[k, 0:2]),
+            (zonal.at[:, k, :], fields.at[k, 2]),
+            (merid.at[:, k, :], fields.at[k, 3]),
+            (vertical.at[:, k, :], fields.at[k, 4]),
+            (diffusivity.at[:, k, :], fields.at[k, 5]),
+            (turbulence.at[:, turned, :], fields.at[k, 6]),
         ]
-        return [pltpu.make_async_copy(a, b, sems.at[i, k]) for i, (a, b) in enumerate(pairs)]
+        return [pltpu.make_async_copy(a, b, sems.at[k]) for a, b in pairs]
+
+    def arrive(k):
+        pltpu.make_async_copy(fields.at[k], fields.at[k], sems.at[k]).wait()
 
     for k in range(AHEAD):
         for copy in copies(k):
@@ -165,14 +169,13 @@
     grads_kept[0] = jnp.zeros((2, X, Y), F32)
 
     for k in range(2):
-        for copy in copies(k):
-            copy.wait()
-    for t in range(2):
-        grads_kept[1, t] = jnp.where(base + 1 < depth, q[t, 1] - q[t, 0], 0.0)
+        arrive(k)
+    for t in range(2):
+        grads_kept[1, t] = jnp.where(base + 1 < depth, fields[1, t] - fields[0, t], 0.0)
 
     def eliminate(j, tail, prev_rate):
         face = jnp.where(slab == 0, j + 1, 2 * K - 1 - j)
-        turb = tb[j]
+        turb = fields[j, 6]
         next_rate = jnp.where(face < depth, turb * lax.rsqrt(turb), 0.0)
         rest = 1.0 + prev_rate * tail
         inverse = reciprocal(rest + next_rate)
@@ -185,26 +188,26 @@
         ahead = jnp.minimum(k + 2, K - 1)
         level = base + k
         down = jnp.minimum(k + 1, K - 1)
-        here = [q[t, k] for t in range(2)]
-        next_row = [q[t, down] for t in range(2)]
+        here = [fields[k, t] for t in range(2)]
+        next_row = [fields[down, t] for t in range(2)]
         open_far = jnp.where(k < K - 2, level + 2, FAR) < depth
-        grad_far = [jnp.where(open_far, q[t, ahead] - next_row[t], 0.0) for t in range(2)]
+        grad_far = [jnp.where(open_far, fields[ahead, t] - next_row[t], 0.0) for t in range(2)]
         centred = [grad_up[t] + grad_down[t] for t in range(2)]
         known = jnp.where(slab == 0, k < K - 2, k > 0)
         open_flux = jnp.where(known, level + 1, FAR) < depth
-        down_courant = jnp.where(open_flux, vc[down], 0.0)
+        down_courant = jnp.where(open_flux, fields[down, 4], 0.0)
         vert = face_flux(down_courant, here, grad_down, grad_up, grad_far)
         total = []
         for t in range(2):
             total.append(here[t] + below[t] - vert[t])
         iso_level = jnp.where(k == edge, FAR, level)
-        spread = df[k]
+        spread = fields[k, 5]
 
         open_west = level < depth_west
         behind = [row_roll(here[t], 1) for t in range(2)]
         grad = [jnp.where(open_west, here[t] - behind[t], 0.0) for t in range(2)]
         flux = face_flux(
-            jnp.where(level < depth_west_inner, zc[k], 0.0),
+            jnp.where(level < depth_west_inner, fields[k, 2], 0.0),
             behind,
             grad,
             [row_roll(grad[t], 1) for t in range(2)],
@@ -223,7 +226,7 @@
         behind = [lane_roll(here[t], 1) for t in range(2)]
         grad = [jnp.where(open_south, here[t] - behind[t], 0.0) for t in range(2)]
         flux = face_flux(
-            jnp.where(open_south, mc[k], 0.0),
+            jnp.where(open_south, fields[k, 3], 0.0),
             behind,
             grad,
             [lane_roll(grad[t], 1) for t in range(2)],
@@ -248,8 +251,7 @@
                 for copy in copies(first + u + AHEAD):
                     copy.start()
             if wait:
-                for copy in copies(first + u + 2):
-                    copy.wait()
+                arrive(first + u + 2)
         below = [below_flux[t] for t in range(2)]
         grads = [[grads_kept[f, t] for t in range(2)] for f in range(2)]
         tail, prev_rate = tail_out[0], tail_out[1]
@@ -279,11 +281,11 @@
     step(steps - 1, False, False)
     for t in range(2):
         for i in range(3):
-            own_rows[t, i] = q[t, (K - 3) * (1 - slab) + i]
-    extra_rows[0] = vc[edge]
-    extra_rows[1] = vc[1]
-    extra_rows[2] = df[edge]
-    extra_rows[3] = tb[K - 1]
+            own_rows[t, i] = fields[(K - 3) * (1 - slab) + i, t]
+    extra_rows[0] = fields[edge, 4]
+    extra_rows[1] = fields[1, 4]
+    extra_rows[2] = fields[edge, 5]
+    extra_rows[3] = fields[K - 1, 6]
     for copy in column_copies:
         copy.wait()
 
@@ -537,7 +539,7 @@
     edge = (K - 1) * (1 - slab)
 
     def copies(k):
-        return [pltpu.make_async_copy(u.at[t, k], out.at[t, :, k, :], sems.at[t, k]) for t in range(2)]
+        return [pltpu.make_async_copy(u.at[:, k], out.at[:, :, k, :], sems.at[k])]
 
     for t in range(2):
         u[t, edge] = last[t]
@@ -601,18 +603,13 @@
             shape(2, 6, K, Y), shape(3, K, Y), shape(3, K, Y), shape(2, 3, X, Y), shape(4, X, Y),
         ],
         scratch_shapes=[
-            pltpu.VMEM((2, K, X, Y), F32),
-            pltpu.VMEM((K, X, Y), F32),
-            pltpu.VMEM((K, X, Y), F32),
-            pltpu.VMEM((K, X, Y), F32),
-            pltpu.VMEM((K, X, Y), F32),
-            pltpu.VMEM((K, X, Y), F32),
+            pltpu.VMEM((K, 7, X, Y), F32),
             pltpu.VMEM((2, X, Y), F32),
             pltpu.VMEM((2, 2, X, Y), F32),
-            pltpu.SemaphoreType.DMA((6, K)),
+            pltpu.SemaphoreType.DMA((K,)),
             pltpu.SemaphoreType.DMA((18,)),
         ],
-        compiler_params=params(48),
+        compiler_params=params(49),
         cost_estimate=pl.CostEstimate(flops=50_000_000, bytes_accessed=40_000_000, transcendentals=0),
     )(tracers, zonal, merid, vertical, diffusivity, turbulence, sea, bottom)
 
@@ -641,7 +638,7 @@
             pltpu.VMEM((2, K, X, Y), F32),
             pltpu.VMEM((6, 8, Y), F32),
             pltpu.VMEM((2, 2, X, Y), F32),
-            pltpu.SemaphoreType.DMA((2, K)),
+            pltpu.SemaphoreType.DMA((K,)),
         ],
         compiler_params=params(46),
     )(v_first, v_second, ratio, meet, meet_in, corner)

time: 34 us -> 31.7 us (0.932)
  Pallas kernels: 17.7 us -> 15.3 us
    pallas_call x1, Pallas kernels: 11 us -> 9.01 us  [local(): pl.pallas_call(interior_kernel, name='interior', in_specs=[any_spec()] *...]
    pallas_call x1, Pallas kernels: 2.06 us -> 1.63 us  [local(): pl.pallas_call(finish_kernel, name='finish', in_specs=[vmem_spec()] * 6,...]
  transfers between devices with their start and end apart: 4 -> 4, of which waited for: 1 -> 1; matrix products, arithmetic and copies ran while one was open for 0% -> 0% of each run, Pallas kernels for 32% -> 29%
where the time goes in v3:
time: 31.7 us; the launch traced here: 31.4 us
  Pallas kernels  15.3 us (48%)
  starting transfers between devices  10.6 us (33%)
  waiting for transfers between devices  5.34 us (17%)
    pallas_call x1, Pallas kernels, local(): pl.pallas_call(interior_kernel, name='interior', in_specs=[any_spec()] *...  9.01 us
    ppermute x1, starting transfers between devices, local(): west_in = lax.ppermute(west_msg, 'tile', [(b, a) for a, b in eastward])  7.01 us
    ppermute x1, waiting for transfers between devices, local(): meet_in = lax.ppermute(meet, 'lev', [(0, 1), (1, 0)])  5.33 us
    pallas_call x1, Pallas kernels, local(): pl.pallas_call(pack_kernel, name='pack', in_specs=[any_spec()] * 5 + [vme...  2.9 us
    ppermute x1, starting transfers between devices, local(): level_in = lax.ppermute(level_msg, 'lev', [(0, 1), (1, 0)])  2.73 us
    pallas_call x1, Pallas kernels, local(): pl.pallas_call(edge_kernel, name='edges', in_specs=[vmem_spec()] * 15, ou...  1.79 us
    pallas_call x1, Pallas kernels, local(): pl.pallas_call(finish_kernel, name='finish', in_specs=[vmem_spec()] * 6,...  1.63 us
    ppermute x1, starting transfers between devices, local(): meet_in = lax.ppermute(meet, 'lev', [(0, 1), (1, 0)])  0.87 us
  transfers between devices with their start and end apart: 4, of which 1 were waited for; matrix products, arithmetic and copies ran while one was open for 0% of the time, Pallas kernels for 29%

profile of v3, /device:TPU:0, one launch (start us, length us, event | category | flops | bytes accessed | tf_op | source)
XLA Modules:
  0.0 31.4 jit_solution(17975373725248452762)
XLA Ops:
  0.0 0.0 copy-start.1
  0.0 0.0 copy-start
  0.0 2.9 %pack.1 = (f32[136,384]{1,0:T(8,128)}, f32[200,384]{1,0:T(8,128)}, f32[5,16,384]{2,1,0:T(8,128)}) custom-call(f32[2,16,32,384]{3,2,1,0:T(8,128)} %tracers.3, f32[16,32,384]{2,1,0:T(8,128)} %zonal.3, f32[16,32,384]{2,1,0:T(8,128)} %vertical.3, f32[16,32,384]{2,1,0:T(8,128)} %diffusivity.3, f32[16,32,384]{2,1,0:T(8,128)} %turbulence.3, s32[16,384]{1,0:T(8,128)} %sea.5, ...), custom_call_target="tpu_custom_call" | custom-call | tf_op jit(solution)/shard_map/pack/pallas_call | solution.py:580
  2.9 7.0 %collective-permute-start.1 = (f32[200,384]{1,0:T(8,128)}, f32[200,384]{1,0:T(8,128)S(1)}, u32[]{:S(2)}, u32[]{:S(2)}) collective-permute-start(f32[200,384]{1,0:T(8,128)} %get-tuple-element.24), channel_id=1, source_target_pairs={{2,0},{4,2},{6,4},{8,6},{10,8},{12,10},{14,12},{16,14},{18,16},{20... | collective-permute-start | bytes 921608 | tf_op jit(solution)/shard_map/ppermute | solution.py:592
  9.9 0.0 collective-permute-start
  9.9 2.7 %collective-permute-start.2 = (f32[5,16,384]{2,1,0:T(8,128)}, f32[5,16,384]{2,1,0:T(8,128)S(1)}, u32[]{:S(2)}, u32[]{:S(2)}) collective-permute-start(f32[5,16,384]{2,1,0:T(8,128)} %get-tuple-element.25), channel_id=1, source_target_pairs={{0,1},{1,0},{2,3},{3,2},{4,5},{5,4},{6,7},{7,6},{8,9},{9,8},{10,11... | collective-permute-start | bytes 368648 | tf_op jit(solution)/shard_map/ppermute | solution.py:593
  12.7 0.0 copy-done.1
  12.7 0.0 copy-done
  12.7 9.0 %interior.1 = (f32[3,512,128]{2,1,0:T(8,128)S(1)}, f32[3,512,128]{2,1,0:T(8,128)S(1)}, f32[32,16,384]{2,1,0:T(8,128)S(1)}, f32[32,16,384]{2,1,0:T(8,128)S(1)}, f...) custom-call(f32[2,16,32,384]{3,2,1,0:T(8,128)} %tracers.3, ...), custom_call_target="tpu_custom_call" | custom-call | flops 50000000 | bytes 40000000 | tf_op jit(solution)/shard_map/interior/pallas_call | solution.py:595
  21.7 0.0 collective-permute-done.2.level_msg
  21.7 0.0 collective-permute-done.east_msg
  21.7 0.0 collective-permute-done.1.west_msg
  21.7 1.8 %edges.1 = (f32[32,16,384]{2,1,0:T(8,128)S(1)}, f32[32,16,384]{2,1,0:T(8,128)S(1)}, f32[4,16,384]{2,1,0:T(8,128)S(1)}, f32[5,8,384]{2,1,0:T(8,128)S(1)}) custom-call(f32[136,384]{1,0:T(8,128)S(1)} %collective-permute-done.east_msg, f32[200,384]{1,0:T(8,128)S(1)} %collective-permute-done.1.west_msg, f32[5,16,384]{2,1,0:T(8,128)S(1)} %collective-permute-done.2.level_msg, ...), custom_call_target="tpu_custom_call" | custom-call | tf_op jit(solution)/shard_map/edges/pallas_call | solution.py:616
  23.5 0.9 %collective-permute-start.3 = (f32[4,16,384]{2,1,0:T(8,128)S(1)}, f32[4,16,384]{2,1,0:T(8,128)S(1)}, u32[]{:S(2)}, u32[]{:S(2)}) collective-permute-start(f32[4,16,384]{2,1,0:T(8,128)S(1)} %get-tuple-element.39.mine), channel_id=1, source_target_pairs={{0,1},{1,0},{2,3},{3,2},{4,5},{5,4},{6,7},{7,6},{8,9},{9,8},{10,11... | collective-permute-start | bytes 294920 | tf_op jit(solution)/shard_map/ppermute | solution.py:630
  24.4 5.3 %collective-permute-done.3.theirs = f32[4,16,384]{2,1,0:T(8,128)S(1)} collective-permute-done((f32[4,16,384]{2,1,0:T(8,128)S(1)}, f32[4,16,384]{2,1,0:T(8,128)S(1)}, u32[]{:S(2)}, u32[]{:S(2)}) %collective-permute-start.3) | collective-permute-done | bytes 98336 | tf_op jit(solution)/shard_map/ppermute | solution.py:630
  29.7 1.6 %finish.1 = f32[2,16,32,384]{3,2,1,0:T(8,128)} custom-call(f32[32,16,384]{2,1,0:T(8,128)S(1)} %get-tuple-element.36.v_first, f32[32,16,384]{2,1,0:T(8,128)S(1)} %get-tuple-element.37.v_second, f32[32,16,384]{2,1,0:T(8,128)S(1)} %get-tuple-element.38.ratio, f32[4,16,384]{2,1,0:T(8,128)S(1)} %get-tuple-element.39.mine, ...), custom_call_target="tpu_custom_call" | custom-call | tf_op jit(solution)/shard_map/finish/pallas_call | solution.py:631
Async XLA Ops:
  0.0 12.7 %copy-start.1 = (s32[16,384]{1,0:T(8,128)S(1)}, s32[16,384]{1,0:T(8,128)}, u32[]{:S(2)}) copy-start(s32[16,384]{1,0:T(8,128)} %bottom.5) | copy-start | bytes 73732
  0.0 12.7 %copy-start = (s32[16,384]{1,0:T(8,128)S(1)}, s32[16,384]{1,0:T(8,128)}, u32[]{:S(2)}) copy-start(s32[16,384]{1,0:T(8,128)} %sea.5) | copy-start | bytes 73732
  2.9 18.8 %collective-permute-start.1 = (f32[200,384]{1,0:T(8,128)}, f32[200,384]{1,0:T(8,128)S(1)}, u32[]{:S(2)}, u32[]{:S(2)}) collective-permute-start(f32[200,384]{1,0:T(8,128)} %get-tuple-element.24), channel_id=1, source_target_pairs={{2,0},{4,2},{6,4},{8,6},{10,8},{12,10},{14,12},{16,14},{18,16},{20... | collective-permute-start | bytes 921608 | tf_op jit(solution)/shard_map/ppermute | solution.py:592
  9.9 11.8 %collective-permute-start = (f32[136,384]{1,0:T(8,128)}, f32[136,384]{1,0:T(8,128)S(1)}, u32[]{:S(2)}, u32[]{:S(2)}) collective-permute-start(f32[136,384]{1,0:T(8,128)} %get-tuple-element.23), channel_id=1, source_target_pairs={{0,2},{2,4},{4,6},{6,8},{8,10},{10,12},{12,14},{14,16},{16,18},{18... | collective-permute-start | bytes 626696 | tf_op jit(solution)/shard_map/ppermute | solution.py:591
  9.9 11.8 %collective-permute-start.2 = (f32[5,16,384]{2,1,0:T(8,128)}, f32[5,16,384]{2,1,0:T(8,128)S(1)}, u32[]{:S(2)}, u32[]{:S(2)}) collective-permute-start(f32[5,16,384]{2,1,0:T(8,128)} %get-tuple-element.25), channel_id=1, source_target_pairs={{0,1},{1,0},{2,3},{3,2},{4,5},{5,4},{6,7},{7,6},{8,9},{9,8},{10,11... | collective-permute-start | bytes 368648 | tf_op jit(solution)/shard_map/ppermute | solution.py:593
  23.5 6.2 %collective-permute-start.3 = (f32[4,16,384]{2,1,0:T(8,128)S(1)}, f32[4,16,384]{2,1,0:T(8,128)S(1)}, u32[]{:S(2)}, u32[]{:S(2)}) collective-permute-start(f32[4,16,384]{2,1,0:T(8,128)S(1)} %get-tuple-element.39.mine), channel_id=1, source_target_pairs={{0,1},{1,0},{2,3},{3,2},{4,5},{5,4},{6,7},{7,6},{8,9},{9,8},{10,11... | collective-permute-start | bytes 294920 | tf_op jit(solution)/shard_map/ppermute | solution.py:630

commit v4 on v3

--- a/solution.py
+++ b/solution.py
@@ -14,7 +14,7 @@
 Y = 384
 LANES = 3
 UNROLL = 2
-AHEAD = 8
+AHEAD = 12
 FAR = 1 << 20
 F32 = jnp.float32
 
@@ -77,10 +77,15 @@
 
 def pack_kernel(
     tracers, zonal, vertical, diffusivity, turbulence, sea, bottom,
-    east_msg, west_msg, level_msg, depth_rows, sems
+    east_msg, west_msg, level_msg, depth_rows, column, sems
 ):
     slab = lax.axis_index("lev")
     first = (K - 2) * (1 - slab)
+    shapes = [
+        pltpu.make_async_copy(ref, column.at[i], sems.at[20 + i]) for i, ref in enumerate((sea, bottom))
+    ]
+    for copy in shapes:
+        copy.start()
     copies = []
 
     def add(src, dst):
@@ -107,7 +112,9 @@
     def _():
         lower.start()
 
-    depth_rows[...] = (sea[...] * (bottom[...] + 1)).astype(F32)
+    for copy in shapes:
+        copy.wait()
+    depth_rows[...] = (column[0] * (column[1] + 1)).astype(F32)
     last = [
         pltpu.make_async_copy(depth_rows.at[pl.ds(8, 8)], east_msg.at[pl.ds(4 * K, 8)], sems.at[fifth + 1]),
         pltpu.make_async_copy(depth_rows.at[pl.ds(0, 8)], west_msg.at[pl.ds(6 * K, 8)], sems.at[fifth + 2]),
@@ -122,7 +129,7 @@
 def interior_kernel(
     tracers, zonal, merid, vertical, diffusivity, turbulence, sea, bottom,
     p_first, p_second, inverse_out, carry_out, ratio_out, tail_out, cols, zcols, dcols, own_rows, extra_rows,
-    fields, below_flux, grads_kept, sems, col_sems
+    fields, below_flux, grads_kept, column, sems, col_sems
 ):
     slab = lax.axis_index("lev")
     edge = (K - 1) * (1 - slab)
@@ -143,11 +150,18 @@
     def arrive(k):
         pltpu.make_async_copy(fields.at[k], fields.at[k], sems.at[k]).wait()
 
+    shapes = [
+        pltpu.make_async_copy(ref, column.at[i], col_sems.at[18 + i]) for i, ref in enumerate((sea, bottom))
+    ]
+    for copy in shapes:
+        copy.start()
     for k in range(AHEAD):
         for copy in copies(k):
             copy.start()
-
-    depth = sea[...] * (bottom[...] + 1)
+    for copy in shapes:
+        copy.wait()
+
+    depth = column[0] * (column[1] + 1)
     depth_west = west_depth(depth)
     row = lax.broadcasted_iota(jnp.int32, (X, Y), 0)
     depth_west_inner = jnp.where((row >= 2) & (row <= X - 2), depth_west, 0)
@@ -580,10 +594,12 @@
     east_msg, west_msg, level_msg = pl.pallas_call(
         pack_kernel,
         name="pack",
-        in_specs=[any_spec()] * 5 + [vmem_spec()] * 2,
+        in_specs=[any_spec()] * 7,
         out_specs=[vmem_spec()] * 3,
         out_shape=[shape(4 * K + 8, Y), shape(6 * K + 8, Y), shape(5, X, Y)],
-        scratch_shapes=[pltpu.VMEM((X, Y), F32), pltpu.SemaphoreType.DMA((24,))],
+        scratch_shapes=[
+            pltpu.VMEM((X, Y), F32), pltpu.VMEM((2, X, Y), jnp.int32), pltpu.SemaphoreType.DMA((24,))
+        ],
         compiler_params=params(60),
     )(tracers, zonal, vertical, diffusivity, turbulence, sea, bottom)
 
@@ -595,7 +611,7 @@
     p_first, p_second, inverse, carry, ratio, tail, *pieces = pl.pallas_call(
         interior_kernel,
         name="interior",
-        in_specs=[any_spec()] * 6 + [vmem_spec()] * 2,
+        in_specs=[any_spec()] * 8,
         out_specs=[vmem_spec()] * 11,
         out_shape=[
             shape(LANES, K * X, 128), shape(LANES, K * X, 128), shape(K, X, Y), shape(K, X, Y), shape(K, X, Y),
@@ -606,8 +622,9 @@
             pltpu.VMEM((K, 7, X, Y), F32),
             pltpu.VMEM((2, X, Y), F32),
             pltpu.VMEM((2, 2, X, Y), F32),
+            pltpu.VMEM((2, X, Y), jnp.int32),
             pltpu.SemaphoreType.DMA((K,)),
-            pltpu.SemaphoreType.DMA((18,)),
+            pltpu.SemaphoreType.DMA((20,)),
         ],
         compiler_params=params(49),
         cost_estimate=pl.CostEstimate(flops=50_000_000, bytes_accessed=40_000_000, transcendentals=0),

time: 31.7 us -> 30.7 us (0.968)
  Pallas kernels: 15.3 us -> 14.5 us
    pallas_call x1, Pallas kernels: 2.9 us -> 2.12 us  [local(): pl.pallas_call(pack_kernel, name='pack', in_specs=[any_spec()] * 7, out_s...]
where the time goes in v4:
time: 30.7 us; the launch traced here: 30.5 us
  Pallas kernels  14.5 us (47%)
  starting transfers between devices  10.6 us (35%)
  waiting for transfers between devices  5.34 us (17%)
    pallas_call x1, Pallas kernels, local(): pl.pallas_call(interior_kernel, name='interior', in_specs=[any_spec()] *...  8.93 us
    ppermute x1, starting transfers between devices, local(): west_in = lax.ppermute(west_msg, 'tile', [(b, a) for a, b in eastward])  7.02 us
    ppermute x1, waiting for transfers between devices, local(): meet_in = lax.ppermute(meet, 'lev', [(0, 1), (1, 0)])  5.33 us
    ppermute x1, starting transfers between devices, local(): level_in = lax.ppermute(level_msg, 'lev', [(0, 1), (1, 0)])  2.73 us
    pallas_call x1, Pallas kernels, local(): pl.pallas_call(pack_kernel, name='pack', in_specs=[any_spec()] * 7, out_s...  2.12 us
    pallas_call x1, Pallas kernels, local(): pl.pallas_call(edge_kernel, name='edges', in_specs=[vmem_spec()] * 15, ou...  1.79 us
    pallas_call x1, Pallas kernels, local(): pl.pallas_call(finish_kernel, name='finish', in_specs=[vmem_spec()] * 6,...  1.63 us
    ppermute x1, starting transfers between devices, local(): meet_in = lax.ppermute(meet, 'lev', [(0, 1), (1, 0)])  0.87 us
  transfers between devices with their start and end apart: 4, of which 1 were waited for; matrix products, arithmetic and copies ran while one was open for 0% of the time, Pallas kernels for 29%

profile of v4, /device:TPU:0, one launch (start us, length us, event | category | flops | bytes accessed | tf_op | source)
XLA Modules:
  0.0 30.5 jit_solution(8498336966551449766)
XLA Ops:
  0.0 0.0 copy-start.1
  0.0 0.0 copy-start
  0.0 2.1 %pack.1 = (f32[136,384]{1,0:T(8,128)}, f32[200,384]{1,0:T(8,128)}, f32[5,16,384]{2,1,0:T(8,128)}) custom-call(f32[2,16,32,384]{3,2,1,0:T(8,128)} %tracers.3, f32[16,32,384]{2,1,0:T(8,128)} %zonal.3, f32[16,32,384]{2,1,0:T(8,128)} %vertical.3, f32[16,32,384]{2,1,0:T(8,128)} %diffusivity.3, f32[16,32,384]{2,1,0:T(8,128)} %turbulence.3, s32[16,384]{1,0:T(8,128)} %sea.5, ...), custom_call_target="tpu_custom_call" | custom-call | tf_op jit(solution)/shard_map/pack/pallas_call | solution.py:594
  2.1 7.0 %collective-permute-start.1 = (f32[200,384]{1,0:T(8,128)}, f32[200,384]{1,0:T(8,128)S(1)}, u32[]{:S(2)}, u32[]{:S(2)}) collective-permute-start(f32[200,384]{1,0:T(8,128)} %get-tuple-element.24), channel_id=1, source_target_pairs={{2,0},{4,2},{6,4},{8,6},{10,8},{12,10},{14,12},{16,14},{18,16},{20... | collective-permute-start | bytes 921608 | tf_op jit(solution)/shard_map/ppermute | solution.py:608
  9.2 0.0 collective-permute-start
  9.2 2.7 %collective-permute-start.2 = (f32[5,16,384]{2,1,0:T(8,128)}, f32[5,16,384]{2,1,0:T(8,128)S(1)}, u32[]{:S(2)}, u32[]{:S(2)}) collective-permute-start(f32[5,16,384]{2,1,0:T(8,128)} %get-tuple-element.25), channel_id=1, source_target_pairs={{0,1},{1,0},{2,3},{3,2},{4,5},{5,4},{6,7},{7,6},{8,9},{9,8},{10,11... | collective-permute-start | bytes 368648 | tf_op jit(solution)/shard_map/ppermute | solution.py:609
  11.9 0.0 copy-done.1
  11.9 0.0 copy-done
  11.9 8.9 %interior.1 = (f32[3,512,128]{2,1,0:T(8,128)S(1)}, f32[3,512,128]{2,1,0:T(8,128)S(1)}, f32[32,16,384]{2,1,0:T(8,128)S(1)}, f32[32,16,384]{2,1,0:T(8,128)S(1)}, f...) custom-call(f32[2,16,32,384]{3,2,1,0:T(8,128)} %tracers.3, ...), custom_call_target="tpu_custom_call" | custom-call | flops 50000000 | bytes 40000000 | tf_op jit(solution)/shard_map/interior/pallas_call | solution.py:611
  20.8 0.0 collective-permute-done.2.level_msg
  20.8 0.0 collective-permute-done.east_msg
  20.9 0.0 collective-permute-done.1.west_msg
  20.9 1.8 %edges.1 = (f32[32,16,384]{2,1,0:T(8,128)S(1)}, f32[32,16,384]{2,1,0:T(8,128)S(1)}, f32[4,16,384]{2,1,0:T(8,128)S(1)}, f32[5,8,384]{2,1,0:T(8,128)S(1)}) custom-call(f32[136,384]{1,0:T(8,128)S(1)} %collective-permute-done.east_msg, f32[200,384]{1,0:T(8,128)S(1)} %collective-permute-done.1.west_msg, f32[5,16,384]{2,1,0:T(8,128)S(1)} %collective-permute-done.2.level_msg, ...), custom_call_target="tpu_custom_call" | custom-call | tf_op jit(solution)/shard_map/edges/pallas_call | solution.py:633
  22.7 0.9 %collective-permute-start.3 = (f32[4,16,384]{2,1,0:T(8,128)S(1)}, f32[4,16,384]{2,1,0:T(8,128)S(1)}, u32[]{:S(2)}, u32[]{:S(2)}) collective-permute-start(f32[4,16,384]{2,1,0:T(8,128)S(1)} %get-tuple-element.39.mine), channel_id=1, source_target_pairs={{0,1},{1,0},{2,3},{3,2},{4,5},{5,4},{6,7},{7,6},{8,9},{9,8},{10,11... | collective-permute-start | bytes 294920 | tf_op jit(solution)/shard_map/ppermute | solution.py:647
  23.5 5.3 %collective-permute-done.3.theirs = f32[4,16,384]{2,1,0:T(8,128)S(1)} collective-permute-done((f32[4,16,384]{2,1,0:T(8,128)S(1)}, f32[4,16,384]{2,1,0:T(8,128)S(1)}, u32[]{:S(2)}, u32[]{:S(2)}) %collective-permute-start.3) | collective-permute-done | bytes 98336 | tf_op jit(solution)/shard_map/ppermute | solution.py:647
  28.9 1.6 %finish.1 = f32[2,16,32,384]{3,2,1,0:T(8,128)} custom-call(f32[32,16,384]{2,1,0:T(8,128)S(1)} %get-tuple-element.36.v_first, f32[32,16,384]{2,1,0:T(8,128)S(1)} %get-tuple-element.37.v_second, f32[32,16,384]{2,1,0:T(8,128)S(1)} %get-tuple-element.38.ratio, f32[4,16,384]{2,1,0:T(8,128)S(1)} %get-tuple-element.39.mine, ...), custom_call_target="tpu_custom_call" | custom-call | tf_op jit(solution)/shard_map/finish/pallas_call | solution.py:648
Async XLA Ops:
  0.0 11.9 %copy-start.1 = (s32[16,384]{1,0:T(8,128)S(1)}, s32[16,384]{1,0:T(8,128)}, u32[]{:S(2)}) copy-start(s32[16,384]{1,0:T(8,128)} %bottom.5) | copy-start | bytes 73732
  0.0 11.9 %copy-start = (s32[16,384]{1,0:T(8,128)S(1)}, s32[16,384]{1,0:T(8,128)}, u32[]{:S(2)}) copy-start(s32[16,384]{1,0:T(8,128)} %sea.5) | copy-start | bytes 73732
  2.1 18.7 %collective-permute-start.1 = (f32[200,384]{1,0:T(8,128)}, f32[200,384]{1,0:T(8,128)S(1)}, u32[]{:S(2)}, u32[]{:S(2)}) collective-permute-start(f32[200,384]{1,0:T(8,128)} %get-tuple-element.24), channel_id=1, source_target_pairs={{2,0},{4,2},{6,4},{8,6},{10,8},{12,10},{14,12},{16,14},{18,16},{20... | collective-permute-start | bytes 921608 | tf_op jit(solution)/shard_map/ppermute | solution.py:608
  9.2 11.7 %collective-permute-start = (f32[136,384]{1,0:T(8,128)}, f32[136,384]{1,0:T(8,128)S(1)}, u32[]{:S(2)}, u32[]{:S(2)}) collective-permute-start(f32[136,384]{1,0:T(8,128)} %get-tuple-element.23), channel_id=1, source_target_pairs={{0,2},{2,4},{4,6},{6,8},{8,10},{10,12},{12,14},{14,16},{16,18},{18... | collective-permute-start | bytes 626696 | tf_op jit(solution)/shard_map/ppermute | solution.py:607
  9.2 11.7 %collective-permute-start.2 = (f32[5,16,384]{2,1,0:T(8,128)}, f32[5,16,384]{2,1,0:T(8,128)S(1)}, u32[]{:S(2)}, u32[]{:S(2)}) collective-permute-start(f32[5,16,384]{2,1,0:T(8,128)} %get-tuple-element.25), channel_id=1, source_target_pairs={{0,1},{1,0},{2,3},{3,2},{4,5},{5,4},{6,7},{7,6},{8,9},{9,8},{10,11... | collective-permute-start | bytes 368648 | tf_op jit(solution)/shard_map/ppermute | solution.py:609
  22.7 6.2 %collective-permute-start.3 = (f32[4,16,384]{2,1,0:T(8,128)S(1)}, f32[4,16,384]{2,1,0:T(8,128)S(1)}, u32[]{:S(2)}, u32[]{:S(2)}) collective-permute-start(f32[4,16,384]{2,1,0:T(8,128)S(1)} %get-tuple-element.39.mine), channel_id=1, source_target_pairs={{0,1},{1,0},{2,3},{3,2},{4,5},{5,4},{6,7},{7,6},{8,9},{9,8},{10,11... | collective-permute-start | bytes 294920 | tf_op jit(solution)/shard_map/ppermute | solution.py:647

commit v5 on v4

--- a/solution.py
+++ b/solution.py
@@ -14,7 +14,7 @@
 Y = 384
 LANES = 3
 UNROLL = 2
-AHEAD = 12
+AHEAD = 24
 FAR = 1 << 20
 F32 = jnp.float32
 

time: 30.7 us -> 30.3 us (0.987)
  Pallas kernels: 14.5 us -> 14 us
  waiting for transfers between devices: 5.34 us -> 5.03 us
    pallas_call x1, Pallas kernels: 8.93 us -> 8.49 us  [local(): pl.pallas_call(interior_kernel, name='interior', in_specs=[any_spec()] *...]
    ppermute x1, starting transfers between devices: 0.87 us -> 1.18 us  [local(): meet_in = lax.ppermute(meet, 'lev', [(0, 1), (1, 0)])]
    ppermute x1, waiting for transfers between devices: 5.33 us -> 5.02 us  [local(): meet_in = lax.ppermute(meet, 'lev', [(0, 1), (1, 0)])]
  transfers between devices with their start and end apart: 4 -> 4, of which waited for: 1 -> 1; matrix products, arithmetic and copies ran while one was open for 0% -> 0% of each run, Pallas kernels for 29% -> 28%
where the time goes in v5:
time: 30.3 us; the launch traced here: 30.1 us
  Pallas kernels  14 us (46%)
  starting transfers between devices  10.9 us (36%)
  waiting for transfers between devices  5.03 us (17%)
    pallas_call x1, Pallas kernels, local(): pl.pallas_call(interior_kernel, name='interior', in_specs=[any_spec()] *...  8.49 us
    ppermute x1, starting transfers between devices, local(): west_in = lax.ppermute(west_msg, 'tile', [(b, a) for a, b in eastward])  7.02 us
    ppermute x1, waiting for transfers between devices, local(): meet_in = lax.ppermute(meet, 'lev', [(0, 1), (1, 0)])  5.02 us
    ppermute x1, starting transfers between devices, local(): level_in = lax.ppermute(level_msg, 'lev', [(0, 1), (1, 0)])  2.73 us
    pallas_call x1, Pallas kernels, local(): pl.pallas_call(pack_kernel, name='pack', in_specs=[any_spec()] * 7, out_s...  2.12 us
    pallas_call x1, Pallas kernels, local(): pl.pallas_call(edge_kernel, name='edges', in_specs=[vmem_spec()] * 15, ou...  1.79 us
    pallas_call x1, Pallas kernels, local(): pl.pallas_call(finish_kernel, name='finish', in_specs=[vmem_spec()] * 6,...  1.63 us
    ppermute x1, starting transfers between devices, local(): meet_in = lax.ppermute(meet, 'lev', [(0, 1), (1, 0)])  1.18 us
  transfers between devices with their start and end apart: 4, of which 1 were waited for; matrix products, arithmetic and copies ran while one was open for 0% of the time, Pallas kernels for 28%

profile of v5, /device:TPU:0, one launch (start us, length us, event | category | flops | bytes accessed | tf_op | source)
XLA Modules:
  0.0 30.1 jit_solution(10994835094166783531)
XLA Ops:
  0.0 0.0 copy-start.1
  0.0 0.0 copy-start
  0.0 2.1 %pack.1 = (f32[136,384]{1,0:T(8,128)}, f32[200,384]{1,0:T(8,128)}, f32[5,16,384]{2,1,0:T(8,128)}) custom-call(f32[2,16,32,384]{3,2,1,0:T(8,128)} %tracers.3, f32[16,32,384]{2,1,0:T(8,128)} %zonal.3, f32[16,32,384]{2,1,0:T(8,128)} %vertical.3, f32[16,32,384]{2,1,0:T(8,128)} %diffusivity.3, f32[16,32,384]{2,1,0:T(8,128)} %turbulence.3, s32[16,384]{1,0:T(8,128)} %sea.5, ...), custom_call_target="tpu_custom_call" | custom-call | tf_op jit(solution)/shard_map/pack/pallas_call | solution.py:594
  2.1 7.0 %collective-permute-start.1 = (f32[200,384]{1,0:T(8,128)}, f32[200,384]{1,0:T(8,128)S(1)}, u32[]{:S(2)}, u32[]{:S(2)}) collective-permute-start(f32[200,384]{1,0:T(8,128)} %get-tuple-element.24), channel_id=1, source_target_pairs={{2,0},{4,2},{6,4},{8,6},{10,8},{12,10},{14,12},{16,14},{18,16},{20... | collective-permute-start | bytes 921608 | tf_op jit(solution)/shard_map/ppermute | solution.py:608
  9.2 0.0 collective-permute-start
  9.2 2.7 %collective-permute-start.2 = (f32[5,16,384]{2,1,0:T(8,128)}, f32[5,16,384]{2,1,0:T(8,128)S(1)}, u32[]{:S(2)}, u32[]{:S(2)}) collective-permute-start(f32[5,16,384]{2,1,0:T(8,128)} %get-tuple-element.25), channel_id=1, source_target_pairs={{0,1},{1,0},{2,3},{3,2},{4,5},{5,4},{6,7},{7,6},{8,9},{9,8},{10,11... | collective-permute-start | bytes 368648 | tf_op jit(solution)/shard_map/ppermute | solution.py:609
  11.9 0.0 copy-done.1
  11.9 0.0 copy-done
  11.9 8.5 %interior.1 = (f32[3,512,128]{2,1,0:T(8,128)S(1)}, f32[3,512,128]{2,1,0:T(8,128)S(1)}, f32[32,16,384]{2,1,0:T(8,128)S(1)}, f32[32,16,384]{2,1,0:T(8,128)S(1)}, f...) custom-call(f32[2,16,32,384]{3,2,1,0:T(8,128)} %tracers.3, ...), custom_call_target="tpu_custom_call" | custom-call | flops 50000000 | bytes 40000000 | tf_op jit(solution)/shard_map/interior/pallas_call | solution.py:611
  20.4 0.0 collective-permute-done.2.level_msg
  20.4 0.0 collective-permute-done.east_msg
  20.4 0.0 collective-permute-done.1.west_msg
  20.4 1.8 %edges.1 = (f32[32,16,384]{2,1,0:T(8,128)S(1)}, f32[32,16,384]{2,1,0:T(8,128)S(1)}, f32[4,16,384]{2,1,0:T(8,128)S(1)}, f32[5,8,384]{2,1,0:T(8,128)S(1)}) custom-call(f32[136,384]{1,0:T(8,128)S(1)} %collective-permute-done.east_msg, f32[200,384]{1,0:T(8,128)S(1)} %collective-permute-done.1.west_msg, f32[5,16,384]{2,1,0:T(8,128)S(1)} %collective-permute-done.2.level_msg, ...), custom_call_target="tpu_custom_call" | custom-call | tf_op jit(solution)/shard_map/edges/pallas_call | solution.py:633
  22.2 1.2 %collective-permute-start.3 = (f32[4,16,384]{2,1,0:T(8,128)S(1)}, f32[4,16,384]{2,1,0:T(8,128)S(1)}, u32[]{:S(2)}, u32[]{:S(2)}) collective-permute-start(f32[4,16,384]{2,1,0:T(8,128)S(1)} %get-tuple-element.39.mine), channel_id=1, source_target_pairs={{0,1},{1,0},{2,3},{3,2},{4,5},{5,4},{6,7},{7,6},{8,9},{9,8},{10,11... | collective-permute-start | bytes 294920 | tf_op jit(solution)/shard_map/ppermute | solution.py:647
  23.4 5.0 %collective-permute-done.3.theirs = f32[4,16,384]{2,1,0:T(8,128)S(1)} collective-permute-done((f32[4,16,384]{2,1,0:T(8,128)S(1)}, f32[4,16,384]{2,1,0:T(8,128)S(1)}, u32[]{:S(2)}, u32[]{:S(2)}) %collective-permute-start.3) | collective-permute-done | bytes 98336 | tf_op jit(solution)/shard_map/ppermute | solution.py:647
  28.4 1.6 %finish.1 = f32[2,16,32,384]{3,2,1,0:T(8,128)} custom-call(f32[32,16,384]{2,1,0:T(8,128)S(1)} %get-tuple-element.36.v_first, f32[32,16,384]{2,1,0:T(8,128)S(1)} %get-tuple-element.37.v_second, f32[32,16,384]{2,1,0:T(8,128)S(1)} %get-tuple-element.38.ratio, f32[4,16,384]{2,1,0:T(8,128)S(1)} %get-tuple-element.39.mine, ...), custom_call_target="tpu_custom_call" | custom-call | tf_op jit(solution)/shard_map/finish/pallas_call | solution.py:648
Async XLA Ops:
  0.0 11.9 %copy-start.1 = (s32[16,384]{1,0:T(8,128)S(1)}, s32[16,384]{1,0:T(8,128)}, u32[]{:S(2)}) copy-start(s32[16,384]{1,0:T(8,128)} %bottom.5) | copy-start | bytes 73732
  0.0 11.9 %copy-start = (s32[16,384]{1,0:T(8,128)S(1)}, s32[16,384]{1,0:T(8,128)}, u32[]{:S(2)}) copy-start(s32[16,384]{1,0:T(8,128)} %sea.5) | copy-start | bytes 73732
  2.1 18.3 %collective-permute-start.1 = (f32[200,384]{1,0:T(8,128)}, f32[200,384]{1,0:T(8,128)S(1)}, u32[]{:S(2)}, u32[]{:S(2)}) collective-permute-start(f32[200,384]{1,0:T(8,128)} %get-tuple-element.24), channel_id=1, source_target_pairs={{2,0},{4,2},{6,4},{8,6},{10,8},{12,10},{14,12},{16,14},{18,16},{20... | collective-permute-start | bytes 921608 | tf_op jit(solution)/shard_map/ppermute | solution.py:608
  9.2 11.3 %collective-permute-start = (f32[136,384]{1,0:T(8,128)}, f32[136,384]{1,0:T(8,128)S(1)}, u32[]{:S(2)}, u32[]{:S(2)}) collective-permute-start(f32[136,384]{1,0:T(8,128)} %get-tuple-element.23), channel_id=1, source_target_pairs={{0,2},{2,4},{4,6},{6,8},{8,10},{10,12},{12,14},{14,16},{16,18},{18... | collective-permute-start | bytes 626696 | tf_op jit(solution)/shard_map/ppermute | solution.py:607
  9.2 11.2 %collective-permute-start.2 = (f32[5,16,384]{2,1,0:T(8,128)}, f32[5,16,384]{2,1,0:T(8,128)S(1)}, u32[]{:S(2)}, u32[]{:S(2)}) collective-permute-start(f32[5,16,384]{2,1,0:T(8,128)} %get-tuple-element.25), channel_id=1, source_target_pairs={{0,1},{1,0},{2,3},{3,2},{4,5},{5,4},{6,7},{7,6},{8,9},{9,8},{10,11... | collective-permute-start | bytes 368648 | tf_op jit(solution)/shard_map/ppermute | solution.py:609
  22.2 6.2 %collective-permute-start.3 = (f32[4,16,384]{2,1,0:T(8,128)S(1)}, f32[4,16,384]{2,1,0:T(8,128)S(1)}, u32[]{:S(2)}, u32[]{:S(2)}) collective-permute-start(f32[4,16,384]{2,1,0:T(8,128)S(1)} %get-tuple-element.39.mine), channel_id=1, source_target_pairs={{0,1},{1,0},{2,3},{3,2},{4,5},{5,4},{6,7},{7,6},{8,9},{9,8},{10,11... | collective-permute-start | bytes 294920 | tf_op jit(solution)/shard_map/ppermute | solution.py:647

commit v6 on v5

--- a/solution.py
+++ b/solution.py
@@ -166,6 +166,12 @@
     row = lax.broadcasted_iota(jnp.int32, (X, Y), 0)
     depth_west_inner = jnp.where((row >= 2) & (row <= X - 2), depth_west, 0)
     depth_south = south_depth(depth)
+    below_flux[...] = jnp.zeros_like(below_flux)
+    tail_out[...] = jnp.zeros_like(tail_out)
+    grads_kept[0] = jnp.zeros((2, X, Y), F32)
+
+    for k in range(2):
+        arrive(k)
     column_copies = []
 
     def add(src, dst):
@@ -178,12 +184,6 @@
     for i, x in enumerate((0, 1, X - 1)):
         add(zonal.at[x], zcols.at[i])
         add(diffusivity.at[x], dcols.at[i])
-    below_flux[...] = jnp.zeros_like(below_flux)
-    tail_out[...] = jnp.zeros_like(tail_out)
-    grads_kept[0] = jnp.zeros((2, X, Y), F32)
-
-    for k in range(2):
-        arrive(k)
     for t in range(2):
         grads_kept[1, t] = jnp.where(base + 1 < depth, fields[1, t] - fields[0, t], 0.0)
 

time: 30.3 us -> 30.3 us (level)
  no operation moved by 1% of the time
where the time goes in v6:
time: 30.3 us; the launch traced here: 30.1 us
  Pallas kernels  14 us (46%)
  starting transfers between devices  10.9 us (36%)
  waiting for transfers between devices  5.03 us (17%)
    pallas_call x1, Pallas kernels, local(): pl.pallas_call(interior_kernel, name='interior', in_specs=[any_spec()] *...  8.49 us
    ppermute x1, starting transfers between devices, local(): west_in = lax.ppermute(west_msg, 'tile', [(b, a) for a, b in eastward])  7.02 us
    ppermute x1, waiting for transfers between devices, local(): meet_in = lax.ppermute(meet, 'lev', [(0, 1), (1, 0)])  5.03 us
    ppermute x1, starting transfers between devices, local(): level_in = lax.ppermute(level_msg, 'lev', [(0, 1), (1, 0)])  2.73 us
    pallas_call x1, Pallas kernels, local(): pl.pallas_call(pack_kernel, name='pack', in_specs=[any_spec()] * 7, out_s...  2.12 us
    pallas_call x1, Pallas kernels, local(): pl.pallas_call(edge_kernel, name='edges', in_specs=[vmem_spec()] * 15, ou...  1.79 us
    pallas_call x1, Pallas kernels, local(): pl.pallas_call(finish_kernel, name='finish', in_specs=[vmem_spec()] * 6,...  1.63 us
    ppermute x1, starting transfers between devices, local(): meet_in = lax.ppermute(meet, 'lev', [(0, 1), (1, 0)])  1.18 us
  transfers between devices with their start and end apart: 4, of which 1 were waited for; matrix products, arithmetic and copies ran while one was open for 0% of the time, Pallas kernels for 28%

profile of v6, /device:TPU:0, one launch (start us, length us, event | category | flops | bytes accessed | tf_op | source)
XLA Modules:
  0.0 30.1 jit_solution(3743393865424538576)
XLA Ops:
  0.0 0.0 copy-start.1
  0.0 0.0 copy-start
  0.0 2.1 %pack.1 = (f32[136,384]{1,0:T(8,128)}, f32[200,384]{1,0:T(8,128)}, f32[5,16,384]{2,1,0:T(8,128)}) custom-call(f32[2,16,32,384]{3,2,1,0:T(8,128)} %tracers.3, f32[16,32,384]{2,1,0:T(8,128)} %zonal.3, f32[16,32,384]{2,1,0:T(8,128)} %vertical.3, f32[16,32,384]{2,1,0:T(8,128)} %diffusivity.3, f32[16,32,384]{2,1,0:T(8,128)} %turbulence.3, s32[16,384]{1,0:T(8,128)} %sea.5, ...), custom_call_target="tpu_custom_call" | custom-call | tf_op jit(solution)/shard_map/pack/pallas_call | solution.py:594
  2.1 7.0 %collective-permute-start.1 = (f32[200,384]{1,0:T(8,128)}, f32[200,384]{1,0:T(8,128)S(1)}, u32[]{:S(2)}, u32[]{:S(2)}) collective-permute-start(f32[200,384]{1,0:T(8,128)} %get-tuple-element.24), channel_id=1, source_target_pairs={{2,0},{4,2},{6,4},{8,6},{10,8},{12,10},{14,12},{16,14},{18,16},{20... | collective-permute-start | bytes 921608 | tf_op jit(solution)/shard_map/ppermute | solution.py:608
  9.2 0.0 collective-permute-start
  9.2 2.7 %collective-permute-start.2 = (f32[5,16,384]{2,1,0:T(8,128)}, f32[5,16,384]{2,1,0:T(8,128)S(1)}, u32[]{:S(2)}, u32[]{:S(2)}) collective-permute-start(f32[5,16,384]{2,1,0:T(8,128)} %get-tuple-element.25), channel_id=1, source_target_pairs={{0,1},{1,0},{2,3},{3,2},{4,5},{5,4},{6,7},{7,6},{8,9},{9,8},{10,11... | collective-permute-start | bytes 368648 | tf_op jit(solution)/shard_map/ppermute | solution.py:609
  11.9 0.0 copy-done.1
  11.9 0.0 copy-done
  11.9 8.5 %interior.1 = (f32[3,512,128]{2,1,0:T(8,128)S(1)}, f32[3,512,128]{2,1,0:T(8,128)S(1)}, f32[32,16,384]{2,1,0:T(8,128)S(1)}, f32[32,16,384]{2,1,0:T(8,128)S(1)}, f...) custom-call(f32[2,16,32,384]{3,2,1,0:T(8,128)} %tracers.3, ...), custom_call_target="tpu_custom_call" | custom-call | flops 50000000 | bytes 40000000 | tf_op jit(solution)/shard_map/interior/pallas_call | solution.py:611
  20.4 0.0 collective-permute-done.2.level_msg
  20.4 0.0 collective-permute-done.east_msg
  20.4 0.0 collective-permute-done.1.west_msg
  20.4 1.8 %edges.1 = (f32[32,16,384]{2,1,0:T(8,128)S(1)}, f32[32,16,384]{2,1,0:T(8,128)S(1)}, f32[4,16,384]{2,1,0:T(8,128)S(1)}, f32[5,8,384]{2,1,0:T(8,128)S(1)}) custom-call(f32[136,384]{1,0:T(8,128)S(1)} %collective-permute-done.east_msg, f32[200,384]{1,0:T(8,128)S(1)} %collective-permute-done.1.west_msg, f32[5,16,384]{2,1,0:T(8,128)S(1)} %collective-permute-done.2.level_msg, ...), custom_call_target="tpu_custom_call" | custom-call | tf_op jit(solution)/shard_map/edges/pallas_call | solution.py:633
  22.2 1.2 %collective-permute-start.3 = (f32[4,16,384]{2,1,0:T(8,128)S(1)}, f32[4,16,384]{2,1,0:T(8,128)S(1)}, u32[]{:S(2)}, u32[]{:S(2)}) collective-permute-start(f32[4,16,384]{2,1,0:T(8,128)S(1)} %get-tuple-element.39.mine), channel_id=1, source_target_pairs={{0,1},{1,0},{2,3},{3,2},{4,5},{5,4},{6,7},{7,6},{8,9},{9,8},{10,11... | collective-permute-start | bytes 294920 | tf_op jit(solution)/shard_map/ppermute | solution.py:647
  23.4 5.0 %collective-permute-done.3.theirs = f32[4,16,384]{2,1,0:T(8,128)S(1)} collective-permute-done((f32[4,16,384]{2,1,0:T(8,128)S(1)}, f32[4,16,384]{2,1,0:T(8,128)S(1)}, u32[]{:S(2)}, u32[]{:S(2)}) %collective-permute-start.3) | collective-permute-done | bytes 98336 | tf_op jit(solution)/shard_map/ppermute | solution.py:647
  28.4 1.6 %finish.1 = f32[2,16,32,384]{3,2,1,0:T(8,128)} custom-call(f32[32,16,384]{2,1,0:T(8,128)S(1)} %get-tuple-element.36.v_first, f32[32,16,384]{2,1,0:T(8,128)S(1)} %get-tuple-element.37.v_second, f32[32,16,384]{2,1,0:T(8,128)S(1)} %get-tuple-element.38.ratio, f32[4,16,384]{2,1,0:T(8,128)S(1)} %get-tuple-element.39.mine, ...), custom_call_target="tpu_custom_call" | custom-call | tf_op jit(solution)/shard_map/finish/pallas_call | solution.py:648
Async XLA Ops:
  0.0 11.9 %copy-start.1 = (s32[16,384]{1,0:T(8,128)S(1)}, s32[16,384]{1,0:T(8,128)}, u32[]{:S(2)}) copy-start(s32[16,384]{1,0:T(8,128)} %bottom.5) | copy-start | bytes 73732
  0.0 11.9 %copy-start = (s32[16,384]{1,0:T(8,128)S(1)}, s32[16,384]{1,0:T(8,128)}, u32[]{:S(2)}) copy-start(s32[16,384]{1,0:T(8,128)} %sea.5) | copy-start | bytes 73732
  2.1 18.3 %collective-permute-start.1 = (f32[200,384]{1,0:T(8,128)}, f32[200,384]{1,0:T(8,128)S(1)}, u32[]{:S(2)}, u32[]{:S(2)}) collective-permute-start(f32[200,384]{1,0:T(8,128)} %get-tuple-element.24), channel_id=1, source_target_pairs={{2,0},{4,2},{6,4},{8,6},{10,8},{12,10},{14,12},{16,14},{18,16},{20... | collective-permute-start | bytes 921608 | tf_op jit(solution)/shard_map/ppermute | solution.py:608
  9.2 11.3 %collective-permute-start = (f32[136,384]{1,0:T(8,128)}, f32[136,384]{1,0:T(8,128)S(1)}, u32[]{:S(2)}, u32[]{:S(2)}) collective-permute-start(f32[136,384]{1,0:T(8,128)} %get-tuple-element.23), channel_id=1, source_target_pairs={{0,2},{2,4},{4,6},{6,8},{8,10},{10,12},{12,14},{14,16},{16,18},{18... | collective-permute-start | bytes 626696 | tf_op jit(solution)/shard_map/ppermute | solution.py:607
  9.2 11.2 %collective-permute-start.2 = (f32[5,16,384]{2,1,0:T(8,128)}, f32[5,16,384]{2,1,0:T(8,128)S(1)}, u32[]{:S(2)}, u32[]{:S(2)}) collective-permute-start(f32[5,16,384]{2,1,0:T(8,128)} %get-tuple-element.25), channel_id=1, source_target_pairs={{0,1},{1,0},{2,3},{3,2},{4,5},{5,4},{6,7},{7,6},{8,9},{9,8},{10,11... | collective-permute-start | bytes 368648 | tf_op jit(solution)/shard_map/ppermute | solution.py:609
  22.2 6.2 %collective-permute-start.3 = (f32[4,16,384]{2,1,0:T(8,128)S(1)}, f32[4,16,384]{2,1,0:T(8,128)S(1)}, u32[]{:S(2)}, u32[]{:S(2)}) collective-permute-start(f32[4,16,384]{2,1,0:T(8,128)S(1)} %get-tuple-element.39.mine), channel_id=1, source_target_pairs={{0,1},{1,0},{2,3},{3,2},{4,5},{5,4},{6,7},{7,6},{8,9},{9,8},{10,11... | collective-permute-start | bytes 294920 | tf_op jit(solution)/shard_map/ppermute | solution.py:647
